TPU v7x, 512 devices: a whole 4x4x16 slice. The times are simulated.
512 devices in a mesh: dom: 64 (over z, y), pme: 8 (over x, core).
Axes of the slice: x: 4, y: 4, z: 16, core: 2. Of those that a mesh axis runs over, the one named last changes fastest.
Arguments:
- positions: float32 [1024, 3, 128], P(('dom', 'pme')), may hold values from 0 to 256, as said below
- charges: float32 [1024, 128], P(('dom', 'pme')), may hold values from -1 to 1
- counts: int32 [1024], P(('dom', 'pme')), may hold values from 64 to 128
- mol_ids: int32 [1024, 128], P(('dom', 'pme')), may hold values from 0 to 47
- pair_blocks: int32 [24576, 2], P(('dom', 'pme')), may hold values from 0 to 1, as said below
- pair_count: int32 [512], P(('dom', 'pme')), may hold values from 1 to 48, as said below
Outputs:
- forces: float32 [1024, 3, 128], P(('dom', 'pme'))
Inputs may be any that keep to these rules, and one draw needn't show every extreme that they name: `positions`: atom slots of block b lie in the region of their device e = b // 2 = d * 8 + p: first coordinate in [4 d, 4 (d + 1)), second in [32 p, 32 (p + 1)), third in [k * 128, (k + 1) * 128) with k = b mod 2. `pair_blocks`: each row holds a block number of the device (0 to 1, counted within the device) and a block number of the next device along dom, the two at most one apart. Rows past the device's pair_count are not evaluated. `pair_count`: some device has all 48 slots listed in every draw.
All inputs are finite; a program needn't handle non-finite values.
Results may differ from a plain program's by a relative error of at most 0.0003.
Values sent between devices are 32-bit elements; how exact they have to be, the bound alone decides.
A program may use at most 64 MiB of HBM per device.

v0:
```python
import math

import jax
import jax.numpy as jnp
from jax import lax
from jax.sharding import PartitionSpec as P

GRID = 256
GZ = 256


coulomb = 8.0
ewald_beta = 1.0
softening = 1.0
sigma_six = 2.5**6
well_depth = 0.5
core_alpha = 0.5
recip_scale = 6.0
group_pairs = 8
highest = lax.Precision.HIGHEST


def with_halo(cells, sides, width):
    for axis, dim in sides:
        count = lax.axis_size(axis)
        head = lax.slice_in_dim(cells, 0, width, axis=dim)
        tail = lax.slice_in_dim(cells, cells.shape[dim] - width, cells.shape[dim], axis=dim)
        cells = jnp.concatenate(
            [
                lax.ppermute(tail, axis, [(i, (i + 1) % count) for i in range(count)]),
                cells,
                lax.ppermute(head, axis, [((i + 1) % count, i) for i in range(count)]),
            ],
            axis=dim,
        )
    return cells


def from_behind(block, axis, distance):
    devices = range(lax.axis_size(axis))
    route = [((i - distance) % len(devices), i) for i in devices]
    return lax.ppermute(block, axis, route)


def spline(t, order):
    total = jnp.zeros_like(t)
    for k in range(order + 1):
        total = total + (-1.0) ** k * math.comb(order, k) * jnp.maximum(t - k, 0.0) ** (order - 1)
    return jnp.where(t < order, total / math.factorial(order - 1), 0.0)


def weights(coord, index, length):
    shift = jnp.mod(coord[None, :] - index[:, None].astype(coord.dtype) + 3.0, length)
    return (spline(shift, 6), spline(shift, 5) - spline(shift - 1.0, 5))


def wrapped(index, length):
    return jnp.where(index < length // 2, index, index - length)


def influence(index_x, index_y, index_z, full_x, full_y, full_z):
    fx = wrapped(index_x, full_x).astype(jnp.float32) / full_x
    fy = wrapped(index_y, full_y).astype(jnp.float32) / full_y
    fz = wrapped(index_z, full_z).astype(jnp.float32) / full_z
    wave = fx * fx + fy * fy + fz * fz
    safe = jnp.where(wave > 0, wave, 1.0)
    return jnp.where(
        wave > 0, recip_scale * jnp.exp(-math.pi**2 * safe / ewald_beta**2) / safe, 0.0
    )


def pair_tile(left, right, grid_len, depth_len):
    parts = []
    for comp, length in ((0, grid_len), (1, grid_len), (2, depth_len)):
        delta = left[..., comp, :, None] - right[..., comp, None, :]
        parts.append(jnp.mod(delta + 0.5 * length, length) - 0.5 * length)
    dist_sq = parts[0] * parts[0] + parts[1] * parts[1] + parts[2] * parts[2]
    charge_prod = left[..., 3, :, None] * right[..., 3, None, :]
    present = left[..., 5, :, None] * right[..., 5, None, :]
    same = (left[..., 4, :, None] == right[..., 4, None, :]).astype(dist_sq.dtype)
    soft_sq = dist_sq + softening
    soft = jnp.sqrt(soft_sq)
    gauss = 2.0 * ewald_beta / math.sqrt(math.pi) * jnp.exp(-(ewald_beta**2) * soft_sq)
    direct = (
        coulomb * charge_prod * (jax.scipy.special.erfc(ewald_beta * soft) / soft + gauss) / soft_sq
    )
    removed = (
        -coulomb * charge_prod * (jax.scipy.special.erf(ewald_beta * soft) / soft - gauss) / soft_sq
    )
    hard = core_alpha * sigma_six + dist_sq**3
    ratio = sigma_six / hard
    dispersion = 24.0 * well_depth * dist_sq * dist_sq * (2.0 * ratio * ratio - ratio) / hard
    scalar = present * (same * removed + (1.0 - same) * (direct + dispersion))
    on_left = jnp.stack([jnp.sum(scalar * piece, axis=-1) for piece in parts], axis=-2)
    on_right = jnp.stack([-jnp.sum(scalar * piece, axis=-2) for piece in parts], axis=-2)
    return (on_left, on_right)


def evaluate(pairs, first, stop, left_atoms, right_atoms):
    blocks = left_atoms.shape[0]
    slots = pairs.shape[0]
    block_ids = jnp.arange(blocks, dtype=jnp.int32)
    rounds = (stop - first + group_pairs - 1) // group_pairs

    def one_round(step, totals):
        index = first + step * group_pairs + jnp.arange(group_pairs, dtype=jnp.int32)
        valid = (index < stop).astype(jnp.float32)
        rows = jnp.take(pairs, jnp.minimum(index, slots - 1), axis=0)
        on_left, on_right = pair_tile(
            jnp.take(left_atoms, rows[:, 0], axis=0),
            jnp.take(right_atoms, rows[:, 1], axis=0),
            GRID,
            GZ,
        )
        pick_left = (rows[:, 0][:, None] == block_ids[None, :]).astype(jnp.float32) * valid[:, None]
        pick_right = (rows[:, 1][:, None] == block_ids[None, :]).astype(jnp.float32) * valid[
            :, None
        ]
        add_left = jnp.einsum("pb,pcn->bcn", pick_left, on_left, precision=highest)
        add_right = jnp.einsum("pb,pcn->bcn", pick_right, on_right, precision=highest)
        return (totals[0] + add_left, totals[1] + add_right)

    empty = jnp.zeros((blocks, 3, left_atoms.shape[2]), jnp.float32)
    return lax.fori_loop(0, rounds, one_round, (empty, empty))


def tables(length):
    index = jnp.arange(length, dtype=jnp.int32)
    angle = 2.0 * math.pi / length * (index[:, None] * index[None, :] % length).astype(jnp.float32)
    return (jnp.cos(angle), jnp.sin(angle))


def offsets():
    return [-1, 0, 1]


def edge_spans(offset, length):
    if offset == 0:
        return [(0, length)]
    if offset < 0:
        return [(0, 3)]
    return [(length - 3, 3)]


def spread_block(mesh, x_weights, y_weights, loaded, x_first, y_first):
    rows_x = x_weights.shape[0]
    rows_y = y_weights.shape[0]
    plane = (x_weights[:, None, :] * y_weights[None, :, :]).reshape(
        rows_x * rows_y, loaded.shape[1]
    )
    part = lax.dot_general(plane, loaded, (((1,), (1,)), ((), ())), precision=highest).reshape(
        rows_x, rows_y, loaded.shape[0]
    )
    return mesh.at[x_first : x_first + rows_x, y_first : y_first + rows_y].add(part)


def per_device(positions, charges, counts, mol_ids, pair_blocks, pair_count):
    blocks = positions.shape[0]
    width = positions.shape[2]
    atoms = blocks * width
    dom_count = lax.axis_size("dom")
    pme_count = lax.axis_size("pme")
    slab_x = GRID // dom_count
    slab_y = GRID // pme_count
    depth_part = GZ // pme_count
    line_part = GRID // dom_count
    dom_pos = lax.axis_index("dom")
    pme_pos = lax.axis_index("pme")
    x_start = dom_pos * slab_x
    y_start = pme_pos * slab_y
    live = (jnp.arange(width, dtype=jnp.int32)[None, :] < counts[:, None]).astype(jnp.float32)
    payload = jnp.concatenate(
        [
            positions,
            (charges * live)[:, None, :],
            mol_ids.astype(jnp.float32)[:, None, :],
            live[:, None, :],
        ],
        axis=1,
    )
    charge = payload[:, 3, :].reshape(-1)
    cells_z = jnp.arange(GZ, dtype=jnp.int32)
    rim_x = jnp.mod(x_start - 3 + jnp.arange(slab_x + 6, dtype=jnp.int32), GRID)
    rim_y = jnp.mod(y_start - 3 + jnp.arange(slab_y + 6, dtype=jnp.int32), GRID)
    wx, dwx = weights(payload[:, 0, :].reshape(-1), rim_x, GRID)
    wy, dwy = weights(payload[:, 1, :].reshape(-1), rim_y, GRID)
    wz, dwz = weights(payload[:, 2, :].reshape(-1), cells_z, GZ)
    size = (slab_x + 6) * (slab_y + 6)
    plane = (wx[:, None, :] * wy[None, :, :]).reshape(size, atoms)
    own_loaded = wz * charge[None, :]
    nearby = with_halo(payload[None, None], (("dom", 0), ("pme", 1)), 1)
    upper_atoms = nearby[2, 1]
    core_x = x_start + jnp.arange(slab_x, dtype=jnp.int32)
    core_y = y_start + jnp.arange(slab_y, dtype=jnp.int32)
    mesh = jnp.zeros((slab_x, slab_y, GZ), jnp.float32)
    for step_dom in offsets():
        for step_pme in offsets():
            if step_dom == 0 and step_pme == 0:
                mesh = spread_block(mesh, wx[3 : slab_x + 3], wy[3 : slab_y + 3], own_loaded, 0, 0)
                continue
            source = nearby[1 + step_dom, 1 + step_pme]
            source_x = source[:, 0, :].reshape(-1)
            source_y = source[:, 1, :].reshape(-1)
            source_z, _ = weights(source[:, 2, :].reshape(-1), cells_z, GZ)
            loaded = source_z * source[:, 3, :].reshape(-1)[None, :]
            y_parts = []
            for y_first, y_rows in edge_spans(step_pme, slab_y):
                y_weights, _ = weights(source_y, core_y[y_first : y_first + y_rows], GRID)
                y_parts.append((y_first, y_weights))
            for x_first, x_rows in edge_spans(step_dom, slab_x):
                x_weights, _ = weights(source_x, core_x[x_first : x_first + x_rows], GRID)
                y_first, y_weights = y_parts[0]
                mesh = spread_block(mesh, x_weights, y_weights, loaded, x_first, y_first)
    listed = pair_count[0]
    own_part, above_part = evaluate(pair_blocks, 0, listed, payload, upper_atoms)
    short_forces = own_part
    short_forces = short_forces + from_behind(above_part, "dom", 1)
    cos_z, sin_z = tables(GZ)
    cos_l, sin_l = tables(GRID)
    freq_x = jnp.arange(GRID, dtype=jnp.int32)[:, None, None]
    freq_z = (pme_pos * depth_part + jnp.arange(depth_part, dtype=jnp.int32))[None, :, None]
    freq_y = (dom_pos * line_part + jnp.arange(line_part, dtype=jnp.int32))[None, None, :]
    kernel = influence(freq_x, freq_y, freq_z, GRID, GRID, GZ).reshape(
        GRID, depth_part * line_part
    ) / (GRID * GRID * GZ)
    spec = jnp.stack(
        [
            jnp.einsum("xyz,zk->xyk", mesh, cos_z, precision=highest),
            -jnp.einsum("xyz,zk->xyk", mesh, sin_z, precision=highest),
        ]
    )
    lines = lax.all_to_all(spec, "pme", split_axis=3, concat_axis=2, tiled=True)
    real_part = jnp.einsum("xyz,yk->xzk", lines[0], cos_l, precision=highest) + jnp.einsum(
        "xyz,yk->xzk", lines[1], sin_l, precision=highest
    )
    imag_part = jnp.einsum("xyz,yk->xzk", lines[1], cos_l, precision=highest) - jnp.einsum(
        "xyz,yk->xzk", lines[0], sin_l, precision=highest
    )
    spec = jnp.stack([real_part, imag_part])
    spec = spec.reshape(2, slab_x, depth_part, dom_count, line_part)
    spec = lax.all_to_all(spec, "dom", split_axis=3, concat_axis=1, tiled=True).reshape(
        2, GRID, depth_part * line_part
    )
    real_part = (
        jnp.dot(cos_l, spec[0], precision=highest) + jnp.dot(sin_l, spec[1], precision=highest)
    ) * kernel
    imag_part = (
        jnp.dot(cos_l, spec[1], precision=highest) - jnp.dot(sin_l, spec[0], precision=highest)
    ) * kernel
    spec = jnp.stack(
        [
            jnp.dot(cos_l, real_part, precision=highest)
            - jnp.dot(sin_l, imag_part, precision=highest),
            jnp.dot(sin_l, real_part, precision=highest)
            + jnp.dot(cos_l, imag_part, precision=highest),
        ]
    )
    spec = spec.reshape(2, GRID, depth_part, 1, line_part)
    spec = lax.all_to_all(spec, "dom", split_axis=1, concat_axis=3, tiled=True).reshape(
        2, slab_x, depth_part, GRID
    )
    real_part = jnp.einsum("xzk,yk->xyz", spec[0], cos_l, precision=highest) - jnp.einsum(
        "xzk,yk->xyz", spec[1], sin_l, precision=highest
    )
    imag_part = jnp.einsum("xzk,yk->xyz", spec[0], sin_l, precision=highest) + jnp.einsum(
        "xzk,yk->xyz", spec[1], cos_l, precision=highest
    )
    spec = jnp.stack([real_part, imag_part])
    lines = lax.all_to_all(spec, "pme", split_axis=2, concat_axis=3, tiled=True)
    potential = jnp.einsum("xyk,zk->xyz", lines[0], cos_z, precision=highest) - jnp.einsum(
        "xyk,zk->xyz", lines[1], sin_z, precision=highest
    )
    padded = with_halo(potential, (("dom", 0), ("pme", 1)), 3)
    flat = padded.reshape(size, GZ)
    along_z = jnp.dot(flat, wz, precision=highest)
    slope_z = jnp.dot(flat, dwz, precision=highest)
    field_x = jnp.sum((dwx[:, None, :] * wy[None, :, :]).reshape(size, atoms) * along_z, axis=0)
    field_y = jnp.sum((wx[:, None, :] * dwy[None, :, :]).reshape(size, atoms) * along_z, axis=0)
    field_z = jnp.sum(plane * slope_z, axis=0)
    mesh_forces = (
        (-charge[None, :] * jnp.stack([field_x, field_y, field_z]))
        .reshape(3, blocks, width)
        .transpose(1, 0, 2)
    )
    return short_forces + mesh_forces


def solution(mesh):
    in_specs = (
        P(("dom", "pme"), None, None),
        P(("dom", "pme"), None),
        P(("dom", "pme")),
        P(("dom", "pme"), None),
        P(("dom", "pme"), None),
        P(("dom", "pme")),
    )
    out_specs = P(("dom", "pme"), None, None)
    return jax.shard_map(
        per_device, mesh=mesh, in_specs=in_specs, out_specs=out_specs, check_vma=False
    )
```

profile of v0, /device:TPU:6, one launch (start us, length us, event | category | flops | bytes accessed | tf_op | source)
XLA Modules:
  0.0 249.1 jit_solution(11884390800234569833)
XLA Ops:
  2.9 13.9 %collective-permute-start = (f32[1,1,2,6,128]{4,3,2,1,0:T(8,128)S(1)}, f32[1,1,2,6,128]{4,3,2,1,0:T(8,128)S(1)}, u32[]{:S(2)}, u32[]{:S(2)}) collective-permute-start(f32[1,1,2,6,128]{4,3,2,1,0:T(8,128)S(1)} %get-tuple-element.446), channel_id=1, source_target_pairs={{8,0},{16,8},{24,16},{32,24},{40,32},{48,40},{56,48},{64,56},{72,6... | collective-permute-start | bytes 18440 | tf_op jit(solution)/shard_map/ppermute | solution.py:32
  16.7 1.9 collective-permute-start.2
  20.2 1.4 and_reduce_fusion
  21.9 3.7 %collective-permute-done.2 = f32[1,1,2,6,128]{4,3,2,1,0:T(8,128)S(1)} collective-permute-done((f32[1,1,2,6,128]{4,3,2,1,0:T(8,128)S(1)}, f32[1,1,2,6,128]{4,3,2,1,0:T(8,128)S(1)}, u32[]{:S(2)}, u32[]{:S(2)}) %collective-permute-start.2) | collective-permute-done | bytes 6176 | tf_op jit(solution)/shard_map/ppermute | solution.py:30
  25.6 1.7 collective-permute-start.4
  27.6 1.3 collective-permute-done.3
  31.3 2.8 %fusion.85 = f32[3,3,256]{2,1,0:T(4,128)S(1)} fusion(f32[256]{0:T(256)S(1)} %bitcast.342, f32[256]{0:T(256)S(1)} %bitcast.343, f32[256]{0:T(256)S(1)} %iota_convert_fusion, f32[4,32,256]{2,1,0:T(8,128)S(1)} %fusion.84, s32[]{:T(128)} %bitcast.20, s32[]{:T(128)} %bitcast.21, f32[3,256]{1,0:T(4,128)S(1)} %get-tuple-element.459, ...), kind=kOutput, calls=%fused_computation.149 | convolution fusion | flops 10820352 | bytes 27657 | tf_op jit(solution)/shard_map/dot_general | solution.py:151
  34.1 1.6 scatter-add.30
  43.8 1.3 fusion.83
  46.3 11.4 %all_to_all.60 = f32[8,1,8192]{2,1,0:T(1,128)S(1)} all-to-all(f32[8,1,8192]{2,1,0:T(1,128)S(1)} %reshape.2349), channel_id=1, replica_groups=mesh['dom'=64,'pme'=8] {'pme'}, dimensions={0} | all-to-all | bytes 524288 | tf_op jit(solution)/shard_map/all_to_all | solution.py:232
  58.2 1.3 reduce.28
  62.3 1.2 fusion.111
  63.5 1.3 convolution_add_fusion.5
  65.0 1.3 convolution_subtract_fusion.4
  66.8 1.4 reshape.2351
  68.1 7.4 %all-to-all-start.1 = ((f32[64,1,1024]{2,1,0:T(1,128)}), f32[64,1,1024]{2,1,0:T(1,128)S(1)}, u32[]{:S(2)}, u32[]{:S(2)}) async-start(f32[64,1,1024]{2,1,0:T(1,128)} %reshape.2351), calls=%async_computation.1 | async-start | bytes 524288 | tf_op jit(solution)/shard_map/all_to_all | solution.py:241
  76.0 21.8 %all-to-all-done.1 = f32[64,1,1024]{2,1,0:T(1,128)S(1)} async-done(((f32[64,1,1024]{2,1,0:T(1,128)}), f32[64,1,1024]{2,1,0:T(1,128)S(1)}, u32[]{:S(2)}, u32[]{:S(2)}) %all-to-all-start.1) | async-done | bytes 262176 | tf_op jit(solution)/shard_map/all_to_all | solution.py:241
  97.8 1.3 reduce.29
  99.7 3.0 %copy.71 = f32[1,64,4,32,1,4]{5,3,2,1,4,0:T(8,128)} copy(f32[1,64,4,32,1,4]{3,5,2,0,1,4:T(4,128)S(1)} %get-tuple-element.396) | data formatting | bytes 262144 | tf_op jit(solution)/shard_map/slice | solution.py:245
  102.8 4.9 %squeeze.85 = f32[256,128]{1,0:T(8,128)S(1)} reshape(f32[1,64,4,32,1,4]{5,3,2,1,4,0:T(8,128)} %copy.71) | data formatting | bytes 262144 | tf_op jit(solution)/shard_map/squeeze | solution.py:245
  107.6 1.6 fusion.750
  109.2 3.0 %copy.70 = f32[1,64,4,32,1,4]{5,3,2,1,4,0:T(8,128)} copy(f32[1,64,4,32,1,4]{3,5,2,0,1,4:T(4,128)S(1)} %get-tuple-element.397) | data formatting | bytes 262144 | tf_op jit(solution)/shard_map/slice | solution.py:245
  112.2 4.9 %squeeze.84 = f32[256,128]{1,0:T(8,128)S(1)} reshape(f32[1,64,4,32,1,4]{5,3,2,1,4,0:T(8,128)} %copy.70) | data formatting | bytes 262144 | tf_op jit(solution)/shard_map/squeeze | solution.py:245
  117.0 2.0 fusion.747
  119.1 1.3 fusion.82
  120.4 1.4 fusion.745
  121.8 1.4 fusion.760
  123.2 1.3 fusion.81
  124.5 1.4 convolution_subtract_fusion.2
  126.2 1.4 convolution_add_fusion.3
  128.8 26.5 %all_to_all.61 = f32[64,1,1024]{2,1,0:T(1,128)S(1)} all-to-all(f32[64,1,1024]{2,1,0:T(1,128)S(1)} %reshape.2353), channel_id=1, replica_groups=mesh['dom'=64,'pme'=8] {'dom'}, dimensions={0} | all-to-all | bytes 524288 | tf_op jit(solution)/shard_map/all_to_all | solution.py:259
  155.3 1.3 reduce.30
  157.7 1.7 fusion.109
  159.4 1.7 fusion.90
  161.5 1.7 fusion.80
  163.2 1.7 fusion.79
  166.1 10.2 %all_to_all.62 = f32[8,1,8192]{2,1,0:T(1,128)S(1)} all-to-all(f32[8,1,8192]{2,1,0:T(1,128)S(1)} %reshape.2355), channel_id=1, replica_groups=mesh['dom'=64,'pme'=8] {'pme'}, dimensions={0} | all-to-all | bytes 524288 | tf_op jit(solution)/shard_map/all_to_all | solution.py:269
  176.2 1.3 reduce.31
  178.9 1.3 fusion.106
  180.5 1.3 convolution_subtract_fusion
  181.8 2.6 %collective-permute-start.5 = (f32[3,32,256]{2,1,0:T(8,128)S(1)}, f32[3,32,256]{2,1,0:T(8,128)S(1)}, u32[]{:S(2)}, u32[]{:S(2)}) collective-permute-start(f32[3,32,256]{2,1,0:T(8,128)S(1)} %get-tuple-element.402), channel_id=1, source_target_pairs={{0,8},{8,16},{16,24},{24,32},{32,40},{40,48},{48,56},{56,64},{64,7... | collective-permute-start | bytes 294920 | tf_op jit(solution)/shard_map/ppermute | solution.py:30
  184.4 6.6 %collective-permute-start.6 = (f32[3,32,256]{2,1,0:T(8,128)S(1)}, f32[3,32,256]{2,1,0:T(8,128)S(1)}, u32[]{:S(2)}, u32[]{:S(2)}) collective-permute-start(f32[3,32,256]{2,1,0:T(8,128)S(1)} %get-tuple-element.403), channel_id=1, source_target_pairs={{8,0},{16,8},{24,16},{32,24},{40,32},{48,40},{56,48},{64,56},{72,6... | collective-permute-start | bytes 294920 | tf_op jit(solution)/shard_map/ppermute | solution.py:32
  193.3 1.7 collective-permute-start.8
  195.0 14.7 %while.27 = (s32[]{:T(128)}, f32[2,3,128]{2,0,1:T(2,128)S(1)}, f32[2,3,128]{2,0,1:T(2,128)S(1)}, s32[]{:T(128)}, s32[48,2]{1,0:T(8,128)S(1)}, /*index=5*/s32[]{:...) while((s32[]{:T(128)}, f32[2,3,128]{2,0,1:T(2,128)S(1)}, ...), condition=%wide.region_7.9_spmd.clone.clone, body=%wide.region_0.8_spmd.clone.clone.sunk | while | flops 17868636 | bytes 443501 | solution.py:124
  197.9 4.1 %fusion.1150 = (f32[8,128]{1,0:T(8,128)S(1)}, f32[8,128]{1,0:T(8,128)S(1)}, f32[8,128]{1,0:T(8,128)S(1)}, f32[8,128]{1,0:T(8,128)S(1)}, f32[8,128]{1,0:T(8,128)S(1)}, /*index=5*/f32[8,128]{1,0:T(8,128)S(1)}) fusion(f32[8,128]{1,0:T(8,128)S(1)} %bitcast.307, f32[8,128]{1,0:T(8,128)S(1)} %bitcast.301, f32[8,128]{1,0:T(8,128)S(1)} %bitcast.305, ...), kind=kLoop, calls=%fused_computation.71.clone.1 | loop fusion | flops 17688576 | bytes 73728 | tf_op jit(solution)/shard_map/while/body/reduce_sum | solution.py:95
  205.3 4.1 %fusion.1150 = (f32[8,128]{1,0:T(8,128)S(1)}, f32[8,128]{1,0:T(8,128)S(1)}, f32[8,128]{1,0:T(8,128)S(1)}, f32[8,128]{1,0:T(8,128)S(1)}, f32[8,128]{1,0:T(8,128)S(1)}, /*index=5*/f32[8,128]{1,0:T(8,128)S(1)}) fusion(f32[8,128]{1,0:T(8,128)S(1)} %bitcast.307, f32[8,128]{1,0:T(8,128)S(1)} %bitcast.301, f32[8,128]{1,0:T(8,128)S(1)} %bitcast.305, ...), kind=kLoop, calls=%fused_computation.71.clone.1 | loop fusion | flops 17688576 | bytes 73728 | tf_op jit(solution)/shard_map/while/body/reduce_sum | solution.py:95
  209.7 1.9 collective-permute-start.1
  214.1 34.3 %collective-permute-done.1 = f32[2,3,128]{2,0,1:T(2,128)S(1)} collective-permute-done((f32[2,3,128]{2,0,1:T(2,128)S(1)}, f32[2,3,128]{2,0,1:T(2,128)S(1)}, u32[]{:S(2)}, u32[]{:S(2)}) %collective-permute-start.1) | collective-permute-done | bytes 3104 | tf_op jit(solution)/shard_map/ppermute | solution.py:42
  (165 shorter events, 38.0 us)
Async XLA Ops:
  2.9 19.1 %collective-permute-start = (f32[1,1,2,6,128]{4,3,2,1,0:T(8,128)S(1)}, f32[1,1,2,6,128]{4,3,2,1,0:T(8,128)S(1)}, u32[]{:S(2)}, u32[]{:S(2)}) collective-permute-start(f32[1,1,2,6,128]{4,3,2,1,0:T(8,128)S(1)} %get-tuple-element.446), channel_id=1, source_target_pairs={{8,0},{16,8},{24,16},{32,24},{40,32},{48,40},{56,48},{64,56},{72,6... | collective-permute-start | bytes 18440 | tf_op jit(solution)/shard_map/ppermute | solution.py:32
  16.7 8.9 %collective-permute-start.2 = (f32[1,1,2,6,128]{4,3,2,1,0:T(8,128)S(1)}, f32[1,1,2,6,128]{4,3,2,1,0:T(8,128)S(1)}, u32[]{:S(2)}, u32[]{:S(2)}) collective-permute-start(f32[1,1,2,6,128]{4,3,2,1,0:T(8,128)S(1)} %get-tuple-element.446), channel_id=1, source_target_pairs={{0,8},{8,16},{16,24},{24,32},{32,40},{40,48},{48,56},{56,64},{64,7... | collective-permute-start | bytes 18440 | tf_op jit(solution)/shard_map/ppermute | solution.py:30
  25.6 3.3 %collective-permute-start.3 = (f32[3,1,2,6,128]{4,3,2,1,0:T(8,128)S(1)}, f32[3,1,2,6,128]{4,3,2,1,0:T(8,128)S(1)}, u32[]{:S(2)}, u32[]{:S(2)}) collective-permute-start(f32[3,1,2,6,128]{4,3,2,1,0:T(8,128)S(1)} %pad_maximum_fusion.8), channel_id=1, source_target_pairs={{0,1},{1,2},{2,3},{3,4},{4,5},{5,6},{6,7},{7,0},{8,9},{9,10},{10,1... | collective-permute-start | bytes 55304 | tf_op jit(solution)/shard_map/ppermute | solution.py:30
  25.6 3.3 %collective-permute-start.4 = (f32[3,1,2,6,128]{4,3,2,1,0:T(8,128)S(1)}, f32[3,1,2,6,128]{4,3,2,1,0:T(8,128)S(1)}, u32[]{:S(2)}, u32[]{:S(2)}) collective-permute-start(f32[3,1,2,6,128]{4,3,2,1,0:T(8,128)S(1)} %pad_maximum_fusion.8), channel_id=1, source_target_pairs={{1,0},{2,1},{3,2},{4,3},{5,4},{6,5},{7,6},{0,7},{9,8},{10,9},{11,1... | collective-permute-start | bytes 55304 | tf_op jit(solution)/shard_map/ppermute | solution.py:32
  68.1 29.6 %all-to-all-start.1 = ((f32[64,1,1024]{2,1,0:T(1,128)}), f32[64,1,1024]{2,1,0:T(1,128)S(1)}, u32[]{:S(2)}, u32[]{:S(2)}) async-start(f32[64,1,1024]{2,1,0:T(1,128)} %reshape.2351), calls=%async_computation.1 | async-start | bytes 524288 | tf_op jit(solution)/shard_map/all_to_all | solution.py:241
  178.7 13.2 %copy-start = (s32[48,2]{0,1:T(2,128)S(1)}, s32[48,2]{0,1:T(2,128)}, u32[]{:S(2)}) copy-start(s32[48,2]{0,1:T(2,128)} %param.34) | copy-start | bytes 1156
  181.8 10.2 %collective-permute-start.5 = (f32[3,32,256]{2,1,0:T(8,128)S(1)}, f32[3,32,256]{2,1,0:T(8,128)S(1)}, u32[]{:S(2)}, u32[]{:S(2)}) collective-permute-start(f32[3,32,256]{2,1,0:T(8,128)S(1)} %get-tuple-element.402), channel_id=1, source_target_pairs={{0,8},{8,16},{16,24},{24,32},{32,40},{40,48},{48,56},{56,64},{64,7... | collective-permute-start | bytes 294920 | tf_op jit(solution)/shard_map/ppermute | solution.py:30
  184.4 8.8 %collective-permute-start.6 = (f32[3,32,256]{2,1,0:T(8,128)S(1)}, f32[3,32,256]{2,1,0:T(8,128)S(1)}, u32[]{:S(2)}, u32[]{:S(2)}) collective-permute-start(f32[3,32,256]{2,1,0:T(8,128)S(1)} %get-tuple-element.403), channel_id=1, source_target_pairs={{8,0},{16,8},{24,16},{32,24},{40,32},{48,40},{56,48},{64,56},{72,6... | collective-permute-start | bytes 294920 | tf_op jit(solution)/shard_map/ppermute | solution.py:32
  193.2 18.4 %collective-permute-start.7 = (f32[10,3,256]{2,1,0:T(4,128)S(1)}, f32[10,3,256]{2,1,0:T(4,128)S(1)}, u32[]{:S(2)}, u32[]{:S(2)}) collective-permute-start(f32[10,3,256]{2,1,0:T(4,128)S(1)} %get-tuple-element.400), channel_id=1, source_target_pairs={{0,1},{1,2},{2,3},{3,4},{4,5},{5,6},{6,7},{7,0},{8,9},{9,10},{10,1... | collective-permute-start | bytes 92168 | tf_op jit(solution)/shard_map/ppermute | solution.py:30
  193.3 18.4 %collective-permute-start.8 = (f32[10,3,256]{2,1,0:T(4,128)S(1)}, f32[10,3,256]{2,1,0:T(4,128)S(1)}, u32[]{:S(2)}, u32[]{:S(2)}) collective-permute-start(f32[10,3,256]{2,1,0:T(4,128)S(1)} %get-tuple-element.401), channel_id=1, source_target_pairs={{1,0},{2,1},{3,2},{4,3},{5,4},{6,5},{7,6},{0,7},{9,8},{10,9},{11,1... | collective-permute-start | bytes 92168 | tf_op jit(solution)/shard_map/ppermute | solution.py:32
  209.7 38.6 %collective-permute-start.1 = (f32[2,3,128]{2,0,1:T(2,128)S(1)}, f32[2,3,128]{2,0,1:T(2,128)S(1)}, u32[]{:S(2)}, u32[]{:S(2)}) collective-permute-start(f32[2,3,128]{2,0,1:T(2,128)S(1)} %get-tuple-element.275), channel_id=1, source_target_pairs={{504,0},{0,8},{8,16},{16,24},{24,32},{32,40},{40,48},{48,56},{56,6... | collective-permute-start | bytes 9224 | tf_op jit(solution)/shard_map/ppermute | solution.py:42
where the time goes:
time: 253 us; the launch traced here: 249 us
  waiting for transfers between devices  62.2 us (25%)
  blocking collectives  48 us (19%)
  matrix products  42.1 us (17%)
  starting transfers between devices  37.7 us (15%)
  local copies, waits for them, and re-layouts  35.6 us (14%)
  other arithmetic  21.5 us (8%)
    ppermute x1, waiting for transfers between devices, from_behind(): return lax.ppermute(block, axis, route)  34.3 us
    all_to_all x1, blocking collectives, per_device(): lax.all_to_all(spec, 'dom', split_axis=1, concat_axis=3, tiled=True)  26.5 us
    ppermute x4, starting transfers between devices, with_halo(): lax.ppermute(head, axis, [((i + 1) % count, i) for i in range(count)])  23.9 us
    all_to_all x1, waiting for transfers between devices, per_device(): lax.all_to_all(spec, 'dom', split_axis=3, concat_axis=1, tiled=True)  21.8 us
    all_to_all x1, blocking collectives, per_device(): lines = lax.all_to_all(spec, 'pme', split_axis=3, concat_axis=2, tiled=True)  11.4 us
    dot_general x9, matrix products, spread_block(): lax.dot_general(plane, loaded, (((1,), (1,)), ((), ())), precision=highest)  10.5 us
    all_to_all x1, blocking collectives, per_device(): lines = lax.all_to_all(spec, 'pme', split_axis=2, concat_axis=3, tiled=True)  10.2 us
    reduce_sum x2, other arithmetic, pair_tile(): jnp.sum(scalar * piece, axis=-2)  8.21 us
  transfers between devices with their start and end apart: 10, of which 5 were waited for; matrix products, arithmetic and copies ran while one was open for 8% of the time, Pallas kernels for 0%

commit v1 on v0

v1 whole, which is shorter than its diff:
```python
import functools
import math

import jax
import jax.numpy as jnp
import ml_dtypes
import numpy as np
from jax import lax
from jax.experimental import pallas as pl
from jax.experimental.pallas import tpu as pltpu
from jax.sharding import PartitionSpec as P

GRID = 256
N_DOM = 64
N_PME = 8
SX = 4
SY = 32
ROWS_Y = 40
FLAT = SX * ROWS_Y
ATOMS = 768
MESH = pl.DeviceIdType.MESH

coulomb = 8.0
sigma_six = 2.5**6
well_depth = 0.5
core_alpha = 0.5
recip_scale = 6.0
f32 = jnp.float32
bf16 = jnp.bfloat16

NN = (((1,), (0,)), ((), ()))
NT = (((1,), (1,)), ((), ()))


def split(value):
    high = value.astype(bf16)
    return high, (value - high.astype(f32)).astype(bf16)


def product(left, right, dims=NN):
    def one(a, b):
        return lax.dot_general(a, b, dims, preferred_element_type=f32)

    return one(left[0], right[0]) + (one(left[0], right[1]) + one(left[1], right[0]))


def swap_groups(pieces):
    group = lax.broadcasted_iota(jnp.int32, pieces[0].shape, 1) // 32
    out = []
    for j in range(4):
        total = pieces[j]
        for i in range(4):
            if i != j:
                total = jnp.where(group == i, pltpu.roll(pieces[i], 32 * ((i - j) % 4), 1), total)
        out.append(total)
    return out


def bumps(delta):
    away = jnp.abs(delta)
    return [jnp.maximum(top - away, 0.0) for top in (3.0, 2.0, 1.0)]


def weight(delta):
    total = 0.0
    for part, factor in zip(bumps(delta), (1.0, -6.0, 15.0)):
        square = part * part
        total = total + (factor / 120.0) * (square * square * part)
    return total


def slope(delta):
    total = 0.0
    for part, factor in zip(bumps(delta), (1.0, -6.0, 15.0)):
        square = part * part
        total = total + (factor / 24.0) * (square * square)
    return jnp.where(delta > 0.0, -total, total)


def depth_delta(coord):
    cells = lax.broadcasted_iota(jnp.int32, (GRID, 128), 0).astype(f32)
    delta = coord - cells
    delta = jnp.where(delta > 128.0, delta - 256.0, delta)
    return jnp.where(delta < -128.0, delta + 256.0, delta)


def scaled_erfc(z):
    t = 1.0 / (1.0 + 0.5 * z)
    poly = 0.17087277
    for c in (
        -0.82215223,
        1.48851587,
        -1.13520398,
        0.27886807,
        -0.18628806,
        0.09678418,
        0.37409196,
        1.00002368,
        -1.26551223,
    ):
        poly = poly * t + c
    return t * jnp.exp(poly)


def pair_scalar(parts, left, right):
    dist_sq = parts[0] * parts[0] + parts[1] * parts[1] + parts[2] * parts[2]
    soft_sq = dist_sq + 1.0
    inv = lax.rsqrt(soft_sq)
    inv_sq = inv * inv
    gauss = jnp.exp(-soft_sq)
    charge = coulomb * left[3] * right[3]
    whole = (
        charge * gauss * (scaled_erfc(soft_sq * inv) * inv + 2.0 / math.sqrt(math.pi)) * inv_sq
    )
    inv_hard = 1.0 / (core_alpha * sigma_six + dist_sq * dist_sq * dist_sq)
    ratio = sigma_six * inv_hard
    dispersion = 24.0 * well_depth * dist_sq * dist_sq * (2.0 * ratio - 1.0) * ratio * inv_hard
    other = jnp.where(left[4] == right[4], -charge * inv * inv_sq, dispersion)
    return left[5] * right[5] * (whole + other)


def kernel(
    pos,
    charges,
    counts,
    mols,
    pairs,
    listed,
    h_hi,
    h_lo,
    y_hi,
    y_lo,
    yt_hi,
    yt_lo,
    out,
    at,
    wz_hi,
    wz_lo,
    dz_hi,
    dz_lo,
    sp,
    rp,
    sd,
    rd,
    sd2,
    rd2,
    sq,
    rq,
    fs,
    fr,
    lam,
    short,
    halo_s,
    halo_r,
    p1_s,
    p1_r,
    d1_s,
    d1_r,
    d2_s,
    d2_r,
    p2_s,
    p2_r,
    f_s,
    f_r,
):
    me_d = lax.axis_index("dom")
    me_p = lax.axis_index("pme")
    up = lax.rem(me_d + 1, N_DOM)
    down = lax.rem(me_d + N_DOM - 1, N_DOM)

    barrier = pltpu.get_barrier_semaphore()

    def greet_pme(k, carry):
        pl.semaphore_signal(
            barrier, inc=1, device_id=(me_d, lax.rem(me_p + k, N_PME)), device_id_type=MESH
        )
        return carry

    def greet_dom(k, carry):
        pl.semaphore_signal(
            barrier, inc=1, device_id=(lax.rem(me_d + k, N_DOM), me_p), device_id_type=MESH
        )
        return carry

    lax.fori_loop(1, N_PME, greet_pme, 0)
    lax.fori_loop(1, N_DOM, greet_dom, 0)

    lane = lax.broadcasted_iota(jnp.int32, (1, 128), 1)
    for b in range(2):
        live = (lane < counts[b]).astype(f32)
        at[1, b, 0:3, :] = pos[b]
        at[1, b, 3:4, :] = charges[b : b + 1, :] * live
        at[1, b, 4:5, :] = mols[b : b + 1, :].astype(f32)
        at[1, b, 5:6, :] = live
        at[1, b, 6:8, :] = jnp.zeros((2, 128), f32)

    pl.semaphore_wait(barrier, N_PME - 1 + N_DOM - 1)

    to_up = pltpu.make_async_remote_copy(
        src_ref=at.at[1],
        dst_ref=at.at[0],
        send_sem=halo_s.at[0],
        recv_sem=halo_r.at[0],
        device_id=(up, me_p),
        device_id_type=MESH,
    )
    to_down = pltpu.make_async_remote_copy(
        src_ref=at.at[1],
        dst_ref=at.at[2],
        send_sem=halo_s.at[1],
        recv_sem=halo_r.at[1],
        device_id=(down, me_p),
        device_id_type=MESH,
    )
    to_up.start()
    to_down.start()

    def depth_weights(side):
        for b in range(2):
            first = (2 * side + b) * 128
            delta = depth_delta(at[side, b, 2:3, :])
            high, low = split(weight(delta) * at[side, b, 3:4, :])
            wz_hi[:, first : first + 128] = high
            wz_lo[:, first : first + 128] = low

    def depth_slopes(side):
        for b in range(2):
            first = (2 * side + b) * 128
            delta = depth_delta(at[side, b, 2:3, :])
            high, low = split(slope(delta) * at[side, b, 3:4, :])
            dz_hi[:, first : first + 128] = high
            dz_lo[:, first : first + 128] = low

    depth_weights(1)
    to_up.wait_recv()
    to_down.wait_recv()
    depth_weights(0)
    depth_weights(2)

    corner_x = (me_d * SX).astype(f32)
    corner_y = (me_p * SY).astype(f32)
    wrap = (
        jnp.where(me_d == 0, 256.0, 0.0).astype(f32),
        f32(0.0),
        jnp.where(me_d == N_DOM - 1, -256.0, 0.0).astype(f32),
    )
    flat_x = jnp.concatenate(
        [at[s, b, 0:1, :] - (wrap[s] + corner_x) for s in range(3) for b in range(2)], axis=1
    )
    flat_y = jnp.concatenate(
        [at[s, b, 1:2, :] - corner_y for s in range(3) for b in range(2)], axis=1
    )
    cells_x = lax.broadcasted_iota(jnp.int32, (8, ATOMS), 0).astype(f32)
    cells_y = lax.broadcasted_iota(jnp.int32, (ROWS_Y, ATOMS), 0).astype(f32) - 3.0
    wx = weight(flat_x - cells_x)
    wy = weight(flat_y - cells_y)

    plane = jnp.concatenate([wx[x : x + 1] * wy for x in range(SX)], axis=0)
    mesh = product(split(plane), (wz_hi[...], wz_lo[...]), NT)
    depth = product(split(mesh), (h_hi[...], h_lo[...]))
    for half in range(2):
        pieces = [
            depth[ROWS_Y * x : ROWS_Y * (x + 1), 128 * half : 128 * (half + 1)] for x in range(SX)
        ]
        for g, piece in enumerate(swap_groups(pieces)):
            sp[4 * half + g] = piece

    def pme_copy(source, target, k, send, receive):
        other = lax.rem(me_p + k, N_PME)
        return pltpu.make_async_remote_copy(
            src_ref=source.at[other],
            dst_ref=target.at[me_p],
            send_sem=send,
            recv_sem=receive,
            device_id=(me_d, other),
            device_id_type=MESH,
        )

    def pme_all(source, target, send, receive):
        return pltpu.make_async_remote_copy(
            src_ref=source.at[pl.ds(0, N_PME - 1)],
            dst_ref=target.at[pl.ds(0, N_PME - 1)],
            send_sem=send,
            recv_sem=receive,
            device_id=(me_d, lax.rem(me_p + 1, N_PME)),
            device_id_type=MESH,
        )

    def dom_copy(source, target, k, send, receive):
        other = lax.rem(me_d + k, N_DOM)
        return pltpu.make_async_remote_copy(
            src_ref=source.at[other],
            dst_ref=target.at[me_d],
            send_sem=send,
            recv_sem=receive,
            device_id=(other, me_p),
            device_id_type=MESH,
        )

    def dom_all(source, target, send, receive):
        return pltpu.make_async_remote_copy(
            src_ref=source.at[pl.ds(0, N_DOM - 1)],
            dst_ref=target.at[pl.ds(0, N_DOM - 1)],
            send_sem=send,
            recv_sem=receive,
            device_id=(up, me_p),
            device_id_type=MESH,
        )

    def start_pme(source, target, send, receive):
        def body(k, carry):
            pme_copy(source, target, k, send, receive).start()
            return carry

        lax.fori_loop(1, N_PME, body, 0)

    def start_dom(source, target, send, receive):
        def body(k, carry):
            dom_copy(source, target, k, send, receive).start()
            dom_copy(source, target, N_DOM - k, send, receive).start()
            return carry

        lax.fori_loop(1, N_DOM // 2, body, 0)
        dom_copy(source, target, N_DOM // 2, send, receive).start()

    start_pme(sp, rp, p1_s, p1_r)
    rp[me_p] = sp[me_p]

    for side in range(3):
        depth_slopes(side)

    pme_all(sp, rp, p1_s, p1_r).wait_recv()
    lines = product(
        (y_hi[...], y_lo[...]), split(rp[...].reshape(N_PME * ROWS_Y, 128))
    )
    flat_sd = sd.reshape(GRID, 128)
    for x, piece in enumerate(swap_groups([lines[64 * k : 64 * (k + 1)] for k in range(4)])):
        flat_sd[pl.ds(x, 64, stride=4), :] = piece
    start_dom(sd, rd, d1_s, d1_r)
    rd[me_d] = sd[me_d]

    def folded(index):
        return jnp.where(index < GRID // 2, index, index - GRID).astype(f32) * (1.0 / GRID)

    lanes = lax.broadcasted_iota(jnp.int32, (GRID, 128), 1)
    freq_x = folded(lax.broadcasted_iota(jnp.int32, (GRID, 128), 0))
    freq_y = folded(me_d * 4 + lanes // 32)
    freq_z = folded(me_p * 32 + lanes % 32)
    wave = freq_x * freq_x + freq_y * freq_y + freq_z * freq_z
    safe = jnp.where(wave > 0.0, wave, 1.0)
    lam[...] = jnp.where(
        wave > 0.0, (recip_scale / GRID**3) * jnp.exp(-(math.pi**2) * safe) / safe, 0.0
    )

    padded = jnp.concatenate([at[1, 0], at[1, 1], jnp.zeros((112, 128), f32)], axis=0)
    columns = padded.T
    rows = lax.broadcasted_iota(jnp.int32, (48, 1), 0)
    sublane = lax.broadcasted_iota(jnp.int32, (128, 128), 1)
    on_own = jnp.zeros((128, 128), f32)
    on_above = [[0.0] * 3, [0.0] * 3]
    for a in range(2):
        left = [columns[:, 8 * a + r : 8 * a + r + 1] for r in range(6)]
        on_left = [0.0] * 3
        for c in range(2):
            right = [at[2, c, r : r + 1, :] for r in range(6)]
            hit = (rows < listed[0]) & (pairs[:, 0:1] == a) & (pairs[:, 1:2] == c)
            times = jnp.sum(hit.astype(f32), axis=0, keepdims=True)
            dz = left[2] - right[2]
            if a < c:
                dz = jnp.where(dz < -128.0, dz + 256.0, dz)
            if a > c:
                dz = jnp.where(dz >= 128.0, dz - 256.0, dz)
            parts = [left[0] - (right[0] - wrap[2]), left[1] - right[1], dz]
            scalar = pair_scalar(parts, left, right) * times
            for v in range(3):
                force = scalar * parts[v]
                on_left[v] = on_left[v] + force
                on_above[c][v] = on_above[c][v] - jnp.sum(force, axis=0, keepdims=True)
        for v in range(3):
            on_own = jnp.where(
                sublane == 3 * a + v, jnp.sum(on_left[v], axis=1, keepdims=True), on_own
            )
    short[0] = on_own.T[0:8]
    short[1] = jnp.concatenate(on_above[0] + on_above[1] + [jnp.zeros((2, 128), f32)], axis=0)

    dom_all(sd, rd, d1_s, d1_r).wait_recv()
    table = (h_hi[...], h_lo[...])
    spectrum = product(table, split(rd.reshape(GRID, 128)[...])) * lam[...]
    sd2.reshape(GRID, 128)[...] = product(table, split(spectrum))
    start_dom(sd2, rd2, d2_s, d2_r)
    rd2[me_d] = sd2[me_d]

    dom_all(sd2, rd2, d2_s, d2_r).wait_recv()
    flat_rd2 = rd2.reshape(GRID, 128)
    lines = jnp.concatenate(
        swap_groups([flat_rd2[pl.ds(x, 64, stride=4), :] for x in range(4)]), axis=0
    )
    sq[...] = product((yt_hi[...], yt_lo[...]), split(lines)).reshape(N_PME, ROWS_Y, 128)
    start_pme(sq, rq, p2_s, p2_r)
    rq[me_p] = sq[me_p]

    dx = slope(flat_x - cells_x)
    dy = slope(flat_y - cells_y)

    pme_all(sq, rq, p2_s, p2_r).wait_recv()
    halves = [swap_groups([rq[4 * half + g] for g in range(4)]) for half in range(2)]
    depth = jnp.concatenate(
        [jnp.concatenate([halves[0][x], halves[1][x]], axis=1) for x in range(SX)], axis=0
    )
    potential = split(product(split(depth), table))
    along = product(potential, (wz_hi[...], wz_lo[...]))
    along_slope = product(potential, (dz_hi[...], dz_lo[...]))
    field = [0.0] * 3
    for x in range(SX):
        here = along[ROWS_Y * x : ROWS_Y * (x + 1)]
        there = along_slope[ROWS_Y * x : ROWS_Y * (x + 1)]
        field[0] = field[0] - dx[x : x + 1] * jnp.sum(wy * here, axis=0, keepdims=True)
        field[1] = field[1] - wx[x : x + 1] * jnp.sum(dy * here, axis=0, keepdims=True)
        field[2] = field[2] - wx[x : x + 1] * jnp.sum(wy * there, axis=0, keepdims=True)

    def force_rows(side):
        return jnp.concatenate(
            [
                field[v][:, 128 * (2 * side + b) : 128 * (2 * side + b + 1)]
                for b in range(2)
                for v in range(3)
            ]
            + [jnp.zeros((2, 128), f32)],
            axis=0,
        )

    fs[0] = force_rows(0)
    fs[1] = force_rows(2) + short[1]
    send_down = pltpu.make_async_remote_copy(
        src_ref=fs.at[0],
        dst_ref=fr.at[0],
        send_sem=f_s.at[0],
        recv_sem=f_r.at[0],
        device_id=(down, me_p),
        device_id_type=MESH,
    )
    send_up = pltpu.make_async_remote_copy(
        src_ref=fs.at[1],
        dst_ref=fr.at[1],
        send_sem=f_s.at[1],
        recv_sem=f_r.at[1],
        device_id=(up, me_p),
        device_id_type=MESH,
    )
    send_down.start()
    send_up.start()
    total = force_rows(1) + short[0]

    to_up.wait_send()
    to_down.wait_send()
    pme_all(sp, rp, p1_s, p1_r).wait_send()
    dom_all(sd, rd, d1_s, d1_r).wait_send()
    dom_all(sd2, rd2, d2_s, d2_r).wait_send()
    pme_all(sq, rq, p2_s, p2_r).wait_send()
    send_down.wait_recv()
    send_up.wait_recv()
    total = total + fr[0] + fr[1]
    out[0] = total[0:3]
    out[1] = total[3:6]
    send_down.wait_send()
    send_up.wait_send()


def two_parts(table):
    high = table.astype(ml_dtypes.bfloat16)
    low = (table - high.astype(np.float64)).astype(ml_dtypes.bfloat16)
    return high, low


def cas(first, second):
    angle = 2.0 * np.pi / GRID * (np.outer(first, second) % GRID)
    return np.cos(angle) + np.sin(angle)


def tables():
    index = np.arange(GRID)
    square = cas(index, index)
    freq = (4 * np.arange(64)[None, :] + np.arange(4)[:, None]).reshape(-1)
    cell = np.arange(ROWS_Y) - 3
    cells = (SY * np.arange(N_PME)[:, None] + cell[None, :]).reshape(-1)
    real = np.tile(np.arange(ROWS_Y) < SY + 6, N_PME)
    lines = cas(freq, cells % GRID) * real[None, :]
    return [*two_parts(square), *two_parts(lines), *two_parts(lines.T)]


def per_device(positions, charges, counts, mol_ids, pair_blocks, pair_count):
    vmem = pl.BlockSpec(memory_space=pltpu.VMEM)
    smem = pl.BlockSpec(memory_space=pltpu.SMEM)
    one = pltpu.SemaphoreType.DMA
    two = pltpu.SemaphoreType.DMA((2,))
    constants = [jnp.asarray(t) for t in tables()]
    return pl.pallas_call(
        kernel,
        out_shape=jax.ShapeDtypeStruct(positions.shape, f32),
        in_specs=[vmem, vmem, smem, vmem, vmem, smem] + [vmem] * 6,
        out_specs=vmem,
        scratch_shapes=[
            pltpu.VMEM((3, 2, 8, 128), f32),
            pltpu.VMEM((GRID, ATOMS), bf16),
            pltpu.VMEM((GRID, ATOMS), bf16),
            pltpu.VMEM((GRID, ATOMS), bf16),
            pltpu.VMEM((GRID, ATOMS), bf16),
            pltpu.VMEM((N_PME, ROWS_Y, 128), f32),
            pltpu.VMEM((N_PME, ROWS_Y, 128), f32),
            pltpu.VMEM((N_DOM, 4, 128), f32),
            pltpu.VMEM((N_DOM, 4, 128), f32),
            pltpu.VMEM((N_DOM, 4, 128), f32),
            pltpu.VMEM((N_DOM, 4, 128), f32),
            pltpu.VMEM((N_PME, ROWS_Y, 128), f32),
            pltpu.VMEM((N_PME, ROWS_Y, 128), f32),
            pltpu.VMEM((2, 8, 128), f32),
            pltpu.VMEM((2, 8, 128), f32),
            pltpu.VMEM((GRID, 128), f32),
            pltpu.VMEM((2, 8, 128), f32),
            two,
            two,
            one,
            one,
            one,
            one,
            one,
            one,
            one,
            one,
            two,
            two,
        ],
        compiler_params=pltpu.CompilerParams(
            collective_id=0, has_side_effects=True, vmem_limit_bytes=40 * 1024 * 1024
        ),
    )(positions, charges, counts, mol_ids, pair_blocks, pair_count, *constants)


def solution(mesh):
    in_specs = (
        P(("dom", "pme"), None, None),
        P(("dom", "pme"), None),
        P(("dom", "pme")),
        P(("dom", "pme"), None),
        P(("dom", "pme"), None),
        P(("dom", "pme")),
    )
    out_specs = P(("dom", "pme"), None, None)
    return jax.shard_map(
        per_device, mesh=mesh, in_specs=in_specs, out_specs=out_specs, check_vma=False
    )
```

time: 253 us -> 70.9 us (0.28)
  the two profiles are of different devices: /device:TPU:6 before, /device:TPU:1 now
where the time goes in v1:
time: 70.9 us; the launch traced here: 70.6 us
  Pallas kernels  62.5 us (88%)
  local copies, waits for them, and re-layouts  7.46 us (11%)
    pallas_call x1, Pallas kernels, per_device(): pl.pallas_call(kernel, out_shape=jax.ShapeDtypeStruct(positions.shape, f3...  62.5 us
    unnamed x22, local copies, waits for them, and re-layouts  6.88 us

profile of v1, /device:TPU:1, one launch (start us, length us, event | category | flops | bytes accessed | tf_op | source)
XLA Modules:
  0.0 70.6 jit_solution(16186937742647627804)
XLA Ops:
  0.7 0.0 copy-start.9
  0.7 0.7 copy.13.pos
  1.4 0.0 copy-done.9
  1.4 0.0 copy-start.6
  1.4 0.0 copy-start.7
  1.4 0.0 copy-start.8
  1.4 0.1 copy.14.pairs
  1.5 0.6 copy-done.6
  2.0 0.0 copy-done.7
  2.1 0.0 copy-done.8
  2.1 0.0 copy-start
  2.1 0.9 %copy-done = bf16[256,320]{1,0:T(8,128)(2,1)S(1)} copy-done((bf16[256,320]{1,0:T(8,128)(2,1)S(1)}, bf16[256,320]{1,0:T(8,128)(2,1)}, u32[]{:S(2)}) %copy-start) | copy-done | bytes 163864
  3.0 0.0 copy-start.1
  3.0 0.9 %copy-done.1 = bf16[256,320]{1,0:T(8,128)(2,1)S(1)} copy-done((bf16[256,320]{1,0:T(8,128)(2,1)S(1)}, bf16[256,320]{1,0:T(8,128)(2,1)}, u32[]{:S(2)}) %copy-start.1) | copy-done | bytes 163864
  3.9 0.0 copy-start.2
  3.9 0.9 %copy-done.2 = bf16[320,256]{1,0:T(8,128)(2,1)S(1)} copy-done((bf16[320,256]{1,0:T(8,128)(2,1)S(1)}, bf16[320,256]{1,0:T(8,128)(2,1)}, u32[]{:S(2)}) %copy-start.2) | copy-done | bytes 163864
  4.8 0.0 copy-start.3
  4.8 0.9 %copy-done.3 = bf16[320,256]{1,0:T(8,128)(2,1)S(1)} copy-done((bf16[320,256]{1,0:T(8,128)(2,1)S(1)}, bf16[320,256]{1,0:T(8,128)(2,1)}, u32[]{:S(2)}) %copy-start.3) | copy-done | bytes 163864
  5.7 0.0 copy-start.4
  5.7 0.9 %copy-done.4 = bf16[256,256]{1,0:T(8,128)(2,1)S(1)} copy-done((bf16[256,256]{1,0:T(8,128)(2,1)S(1)}, bf16[256,256]{1,0:T(8,128)(2,1)}, u32[]{:S(2)}) %copy-start.4) | copy-done | bytes 131096
  6.6 0.0 copy-start.5
  6.7 0.9 %copy-done.5 = bf16[256,256]{1,0:T(8,128)(2,1)S(1)} copy-done((bf16[256,256]{1,0:T(8,128)(2,1)S(1)}, bf16[256,256]{1,0:T(8,128)(2,1)}, u32[]{:S(2)}) %copy-start.5) | copy-done | bytes 131096
  7.6 62.5 %shard_map.118 = f32[2,3,128]{2,1,0:T(4,128)S(1)} custom-call(f32[2,3,128]{2,1,0:T(4,128)S(1)} %copy.13.pos, f32[2,128]{1,0:T(2,128)S(1)} %copy-done.6, s32[2]{0:T(128)S(1)} %copy-done.8, s32[2,128]{1,0:T(2,128)S(1)} %copy-done.7, s32[48,2]{1,0:T(8,128)S(1)} %copy.14.pairs, s32[1]{0:T(128)S(6)} %copy.16.listed, bf16[256,256]{1,0:T(8,128)(2,1)S(1)} %copy-done.5, ...), custom_call_target="tpu_custom_call" | custom-call | tf_op jit(solution)/shard_map/pallas_call | solution.py:497
  70.1 0.6 copy.15
Async XLA Ops:
  0.7 0.7 copy-start.9
  1.4 0.7 copy-start.6
  1.4 0.7 copy-start.7
  1.4 0.7 copy-start.8
  2.1 0.9 %copy-start = (bf16[256,320]{1,0:T(8,128)(2,1)S(1)}, bf16[256,320]{1,0:T(8,128)(2,1)}, u32[]{:S(2)}) copy-start(bf16[256,320]{1,0:T(8,128)(2,1)} %constant.15.clone.y_lo) | copy-start | bytes 491524
  3.0 0.9 %copy-start.1 = (bf16[256,320]{1,0:T(8,128)(2,1)S(1)}, bf16[256,320]{1,0:T(8,128)(2,1)}, u32[]{:S(2)}) copy-start(bf16[256,320]{1,0:T(8,128)(2,1)} %constant.14.clone.y_hi) | copy-start | bytes 491524
  3.9 0.9 %copy-start.2 = (bf16[320,256]{1,0:T(8,128)(2,1)S(1)}, bf16[320,256]{1,0:T(8,128)(2,1)}, u32[]{:S(2)}) copy-start(bf16[320,256]{1,0:T(8,128)(2,1)} %constant.17.clone.yt_lo) | copy-start | bytes 491524
  4.8 0.9 %copy-start.3 = (bf16[320,256]{1,0:T(8,128)(2,1)S(1)}, bf16[320,256]{1,0:T(8,128)(2,1)}, u32[]{:S(2)}) copy-start(bf16[320,256]{1,0:T(8,128)(2,1)} %constant.16.clone.yt_hi) | copy-start | bytes 491524
  5.7 0.9 %copy-start.4 = (bf16[256,256]{1,0:T(8,128)(2,1)S(1)}, bf16[256,256]{1,0:T(8,128)(2,1)}, u32[]{:S(2)}) copy-start(bf16[256,256]{1,0:T(8,128)(2,1)} %constant.13.clone.h_lo) | copy-start | bytes 393220
  6.6 0.9 %copy-start.5 = (bf16[256,256]{1,0:T(8,128)(2,1)S(1)}, bf16[256,256]{1,0:T(8,128)(2,1)}, u32[]{:S(2)}) copy-start(bf16[256,256]{1,0:T(8,128)(2,1)} %constant.12.clone.h_hi) | copy-start | bytes 393220

commit v2 on v1

--- a/solution.py
+++ b/solution.py
@@ -27,6 +27,8 @@
 recip_scale = 6.0
 f32 = jnp.float32
 bf16 = jnp.bfloat16
+
+SPANS = (((0, 144, 0), (240, 256, -256)), ((112, 256, 0), (0, 16, 256)))
 
 NN = (((1,), (0,)), ((), ()))
 NT = (((1,), (1,)), ((), ()))
@@ -75,13 +77,6 @@
         square = part * part
         total = total + (factor / 24.0) * (square * square)
     return jnp.where(delta > 0.0, -total, total)
-
-
-def depth_delta(coord):
-    cells = lax.broadcasted_iota(jnp.int32, (GRID, 128), 0).astype(f32)
-    delta = coord - cells
-    delta = jnp.where(delta > 128.0, delta - 256.0, delta)
-    return jnp.where(delta < -128.0, delta + 256.0, delta)
 
 
 def scaled_erfc(z):
@@ -120,19 +115,26 @@
 
 
 def kernel(
+    pos_in,
+    charges_in,
+    counts_in,
+    mols_in,
+    pairs_in,
+    listed_in,
+    h_in,
+    y_in,
+    yt_in,
+    out,
     pos,
     charges,
     counts,
     mols,
     pairs,
     listed,
-    h_hi,
-    h_lo,
-    y_hi,
-    y_lo,
-    yt_hi,
-    yt_lo,
-    out,
+    h,
+    y,
+    yt,
+    in_s,
     at,
     wz_hi,
     wz_lo,
@@ -168,7 +170,28 @@
     up = lax.rem(me_d + 1, N_DOM)
     down = lax.rem(me_d + N_DOM - 1, N_DOM)
 
+    inputs = [
+        pltpu.make_async_copy(source, target, in_s.at[i])
+        for i, (source, target) in enumerate(
+            (
+                (pos_in, pos),
+                (charges_in, charges),
+                (counts_in, counts),
+                (mols_in, mols),
+                (pairs_in, pairs),
+                (listed_in, listed),
+                (h_in, h),
+                (y_in, y),
+                (yt_in, yt),
+            )
+        )
+    ]
+    for copy in inputs:
+        copy.start()
+
     barrier = pltpu.get_barrier_semaphore()
+    for other in (up, down):
+        pl.semaphore_signal(barrier, inc=1, device_id=(other, me_p), device_id_type=MESH)
 
     def greet_pme(k, carry):
         pl.semaphore_signal(
@@ -183,12 +206,15 @@
         return carry
 
     lax.fori_loop(1, N_PME, greet_pme, 0)
-    lax.fori_loop(1, N_DOM, greet_dom, 0)
-
+    lax.fori_loop(2, N_DOM - 1, greet_dom, 0)
+
+    for copy in inputs[:4]:
+        copy.wait()
     lane = lax.broadcasted_iota(jnp.int32, (1, 128), 1)
     for b in range(2):
         live = (lane < counts[b]).astype(f32)
-        at[1, b, 0:3, :] = pos[b]
+        for v in range(3):
+            at[1, b, v : v + 1, :] = pos[v, b : b + 1, :]
         at[1, b, 3:4, :] = charges[b : b + 1, :] * live
         at[1, b, 4:5, :] = mols[b : b + 1, :].astype(f32)
         at[1, b, 5:6, :] = live
@@ -215,28 +241,24 @@
     to_up.start()
     to_down.start()
 
-    def depth_weights(side):
+    def fill(side, function, high_ref, low_ref):
         for b in range(2):
             first = (2 * side + b) * 128
-            delta = depth_delta(at[side, b, 2:3, :])
-            high, low = split(weight(delta) * at[side, b, 3:4, :])
-            wz_hi[:, first : first + 128] = high
-            wz_lo[:, first : first + 128] = low
-
-    def depth_slopes(side):
-        for b in range(2):
-            first = (2 * side + b) * 128
-            delta = depth_delta(at[side, b, 2:3, :])
-            high, low = split(slope(delta) * at[side, b, 3:4, :])
-            dz_hi[:, first : first + 128] = high
-            dz_lo[:, first : first + 128] = low
-
-    depth_weights(1)
-    to_up.wait_recv()
-    to_down.wait_recv()
-    depth_weights(0)
-    depth_weights(2)
-
+            coord = at[side, b, 2:3, :]
+            charge = at[side, b, 3:4, :]
+            for start, stop, wrap_z in SPANS[b]:
+                cells = lax.broadcasted_iota(jnp.int32, (stop - start, 128), 0)
+                delta = coord - (cells + (start + wrap_z)).astype(f32)
+                high, low = split(function(delta) * charge)
+                high_ref[start:stop, first : first + 128] = high
+                low_ref[start:stop, first : first + 128] = low
+
+    for refs in (wz_hi, wz_lo, dz_hi, dz_lo):
+        for side in range(3):
+            for b in range(2):
+                first = (2 * side + b) * 128
+                refs[128 - 112 * b : 240 - 112 * b, first : first + 128] = jnp.zeros((112, 128), bf16)
+    fill(1, weight, wz_hi, wz_lo)
     corner_x = (me_d * SX).astype(f32)
     corner_y = (me_p * SY).astype(f32)
     wrap = (
@@ -244,20 +266,33 @@
         f32(0.0),
         jnp.where(me_d == N_DOM - 1, -256.0, 0.0).astype(f32),
     )
-    flat_x = jnp.concatenate(
-        [at[s, b, 0:1, :] - (wrap[s] + corner_x) for s in range(3) for b in range(2)], axis=1
-    )
-    flat_y = jnp.concatenate(
-        [at[s, b, 1:2, :] - corner_y for s in range(3) for b in range(2)], axis=1
-    )
-    cells_x = lax.broadcasted_iota(jnp.int32, (8, ATOMS), 0).astype(f32)
-    cells_y = lax.broadcasted_iota(jnp.int32, (ROWS_Y, ATOMS), 0).astype(f32) - 3.0
-    wx = weight(flat_x - cells_x)
-    wy = weight(flat_y - cells_y)
-
-    plane = jnp.concatenate([wx[x : x + 1] * wy for x in range(SX)], axis=0)
-    mesh = product(split(plane), (wz_hi[...], wz_lo[...]), NT)
-    depth = product(split(mesh), (h_hi[...], h_lo[...]))
+    cells_x = lax.broadcasted_iota(jnp.int32, (8, 256), 0).astype(f32)
+    cells_y = lax.broadcasted_iota(jnp.int32, (ROWS_Y, 256), 0).astype(f32) - 3.0
+
+    def deltas(side):
+        flat_x = jnp.concatenate(
+            [at[side, b, 0:1, :] - (wrap[side] + corner_x) for b in range(2)], axis=1
+        )
+        flat_y = jnp.concatenate([at[side, b, 1:2, :] - corner_y for b in range(2)], axis=1)
+        return flat_x - cells_x, flat_y - cells_y
+
+    def spread(side):
+        delta_x, delta_y = deltas(side)
+        wx, wy = weight(delta_x), weight(delta_y)
+        plane = jnp.concatenate([wx[x : x + 1] * wy for x in range(SX)], axis=0)
+        first = 256 * side
+        loaded = (wz_hi[:, first : first + 256], wz_lo[:, first : first + 256])
+        return product(split(plane), loaded, NT)
+
+    mesh = spread(1)
+    to_up.wait_recv()
+    to_down.wait_recv()
+    for side in (0, 2):
+        fill(side, weight, wz_hi, wz_lo)
+        mesh = mesh + spread(side)
+    inputs[6].wait()
+    table = (h[0], h[1])
+    depth = product(split(mesh), table)
     for half in range(2):
         pieces = [
             depth[ROWS_Y * x : ROWS_Y * (x + 1), 128 * half : 128 * (half + 1)] for x in range(SX)
@@ -316,22 +351,23 @@
 
     def start_dom(source, target, send, receive):
         def body(k, carry):
-            dom_copy(source, target, k, send, receive).start()
-            dom_copy(source, target, N_DOM - k, send, receive).start()
+            dom_copy(source, target, N_DOM // 2 - k, send, receive).start()
+            dom_copy(source, target, N_DOM // 2 + k, send, receive).start()
             return carry
 
+        dom_copy(source, target, N_DOM // 2, send, receive).start()
         lax.fori_loop(1, N_DOM // 2, body, 0)
-        dom_copy(source, target, N_DOM // 2, send, receive).start()
 
     start_pme(sp, rp, p1_s, p1_r)
     rp[me_p] = sp[me_p]
 
     for side in range(3):
-        depth_slopes(side)
-
+        fill(side, slope, dz_hi, dz_lo)
+
+    inputs[7].wait()
     pme_all(sp, rp, p1_s, p1_r).wait_recv()
     lines = product(
-        (y_hi[...], y_lo[...]), split(rp[...].reshape(N_PME * ROWS_Y, 128))
+        (y[0], y[1]), split(rp[...].reshape(N_PME * ROWS_Y, 128))
     )
     flat_sd = sd.reshape(GRID, 128)
     for x, piece in enumerate(swap_groups([lines[64 * k : 64 * (k + 1)] for k in range(4)])):
@@ -352,9 +388,17 @@
         wave > 0.0, (recip_scale / GRID**3) * jnp.exp(-(math.pi**2) * safe) / safe, 0.0
     )
 
+    dom_all(sd, rd, d1_s, d1_r).wait_recv()
+    spectrum = product(table, split(rd.reshape(GRID, 128)[...])) * lam[...]
+    sd2.reshape(GRID, 128)[...] = product(table, split(spectrum))
+    start_dom(sd2, rd2, d2_s, d2_r)
+    rd2[me_d] = sd2[me_d]
+
     padded = jnp.concatenate([at[1, 0], at[1, 1], jnp.zeros((112, 128), f32)], axis=0)
     columns = padded.T
-    rows = lax.broadcasted_iota(jnp.int32, (48, 1), 0)
+    inputs[4].wait()
+    inputs[5].wait()
+    rows = lax.broadcasted_iota(jnp.int32, (1, 48), 1)
     sublane = lax.broadcasted_iota(jnp.int32, (128, 128), 1)
     on_own = jnp.zeros((128, 128), f32)
     on_above = [[0.0] * 3, [0.0] * 3]
@@ -363,8 +407,8 @@
         on_left = [0.0] * 3
         for c in range(2):
             right = [at[2, c, r : r + 1, :] for r in range(6)]
-            hit = (rows < listed[0]) & (pairs[:, 0:1] == a) & (pairs[:, 1:2] == c)
-            times = jnp.sum(hit.astype(f32), axis=0, keepdims=True)
+            hit = (rows < listed[0]) & (pairs[0:1, :] == a) & (pairs[1:2, :] == c)
+            times = jnp.sum(hit.astype(f32), axis=1, keepdims=True)
             dz = left[2] - right[2]
             if a < c:
                 dz = jnp.where(dz < -128.0, dz + 256.0, dz)
@@ -383,24 +427,26 @@
     short[0] = on_own.T[0:8]
     short[1] = jnp.concatenate(on_above[0] + on_above[1] + [jnp.zeros((2, 128), f32)], axis=0)
 
-    dom_all(sd, rd, d1_s, d1_r).wait_recv()
-    table = (h_hi[...], h_lo[...])
-    spectrum = product(table, split(rd.reshape(GRID, 128)[...])) * lam[...]
-    sd2.reshape(GRID, 128)[...] = product(table, split(spectrum))
-    start_dom(sd2, rd2, d2_s, d2_r)
-    rd2[me_d] = sd2[me_d]
+    weights_x, slopes_x, weights_y, slopes_y = [], [], [], []
+    for side in range(3):
+        delta_x, delta_y = deltas(side)
+        weights_x.append(weight(delta_x))
+        slopes_x.append(slope(delta_x))
+        weights_y.append(weight(delta_y))
+        slopes_y.append(slope(delta_y))
+    wx, dx, wy, dy = (
+        jnp.concatenate(parts, axis=1) for parts in (weights_x, slopes_x, weights_y, slopes_y)
+    )
+    inputs[8].wait()
 
     dom_all(sd2, rd2, d2_s, d2_r).wait_recv()
     flat_rd2 = rd2.reshape(GRID, 128)
     lines = jnp.concatenate(
         swap_groups([flat_rd2[pl.ds(x, 64, stride=4), :] for x in range(4)]), axis=0
     )
-    sq[...] = product((yt_hi[...], yt_lo[...]), split(lines)).reshape(N_PME, ROWS_Y, 128)
+    sq[...] = product((yt[0], yt[1]), split(lines)).reshape(N_PME, ROWS_Y, 128)
     start_pme(sq, rq, p2_s, p2_r)
     rq[me_p] = sq[me_p]
-
-    dx = slope(flat_x - cells_x)
-    dy = slope(flat_y - cells_y)
 
     pme_all(sq, rq, p2_s, p2_r).wait_recv()
     halves = [swap_groups([rq[4 * half + g] for g in range(4)]) for half in range(2)]
@@ -460,8 +506,9 @@
     send_down.wait_recv()
     send_up.wait_recv()
     total = total + fr[0] + fr[1]
-    out[0] = total[0:3]
-    out[1] = total[3:6]
+    for v in range(3):
+        for b in range(2):
+            out[v, b : b + 1, :] = total[3 * b + v : 3 * b + v + 1]
     send_down.wait_send()
     send_up.wait_send()
 
@@ -469,7 +516,7 @@
 def two_parts(table):
     high = table.astype(ml_dtypes.bfloat16)
     low = (table - high.astype(np.float64)).astype(ml_dtypes.bfloat16)
-    return high, low
+    return np.stack([high, low])
 
 
 def cas(first, second):
@@ -485,21 +532,29 @@
     cells = (SY * np.arange(N_PME)[:, None] + cell[None, :]).reshape(-1)
     real = np.tile(np.arange(ROWS_Y) < SY + 6, N_PME)
     lines = cas(freq, cells % GRID) * real[None, :]
-    return [*two_parts(square), *two_parts(lines), *two_parts(lines.T)]
+    return [two_parts(square), two_parts(lines), two_parts(lines.T)]
 
 
 def per_device(positions, charges, counts, mol_ids, pair_blocks, pair_count):
-    vmem = pl.BlockSpec(memory_space=pltpu.VMEM)
-    smem = pl.BlockSpec(memory_space=pltpu.SMEM)
     one = pltpu.SemaphoreType.DMA
     two = pltpu.SemaphoreType.DMA((2,))
     constants = [jnp.asarray(t) for t in tables()]
-    return pl.pallas_call(
+    forces = pl.pallas_call(
         kernel,
-        out_shape=jax.ShapeDtypeStruct(positions.shape, f32),
-        in_specs=[vmem, vmem, smem, vmem, vmem, smem] + [vmem] * 6,
-        out_specs=vmem,
+        out_shape=pltpu.VMEM((3, 2, 128), f32),
+        in_specs=[pl.BlockSpec(memory_space=pltpu.HBM)] * 9,
+        out_specs=pl.BlockSpec(memory_space=pltpu.VMEM),
         scratch_shapes=[
+            pltpu.VMEM((3, 2, 128), f32),
+            pltpu.VMEM((2, 128), f32),
+            pltpu.SMEM((2,), jnp.int32),
+            pltpu.VMEM((2, 128), jnp.int32),
+            pltpu.VMEM((2, 48), jnp.int32),
+            pltpu.SMEM((1,), jnp.int32),
+            pltpu.VMEM((2, GRID, GRID), bf16),
+            pltpu.VMEM((2, GRID, N_PME * ROWS_Y), bf16),
+            pltpu.VMEM((2, N_PME * ROWS_Y, GRID), bf16),
+            pltpu.SemaphoreType.DMA((9,)),
             pltpu.VMEM((3, 2, 8, 128), f32),
             pltpu.VMEM((GRID, ATOMS), bf16),
             pltpu.VMEM((GRID, ATOMS), bf16),
@@ -531,9 +586,23 @@
             two,
         ],
         compiler_params=pltpu.CompilerParams(
-            collective_id=0, has_side_effects=True, vmem_limit_bytes=40 * 1024 * 1024
+            collective_id=0, has_side_effects=True, vmem_limit_bytes=48 * 1024 * 1024
         ),
-    )(positions, charges, counts, mol_ids, pair_blocks, pair_count, *constants)
+    )(
+        *(
+            value if value is pair_count else pltpu.with_memory_space_constraint(value, pltpu.HBM)
+            for value in (
+                positions.transpose(1, 0, 2),
+                charges,
+                counts,
+                mol_ids,
+                pair_blocks.T,
+                pair_count,
+                *constants,
+            )
+        )
+    )
+    return forces.transpose(1, 0, 2)
 
 
 def solution(mesh):

time: 70.9 us -> 59.1 us (0.83)
  local copies, waits for them, and re-layouts: 7.46 us -> 0.58 us
  Pallas kernels: 62.5 us -> 57.7 us
    unnamed x22 -> x1, local copies, waits for them, and re-layouts: 6.88 us -> 0.58 us
    pallas_call x1, Pallas kernels: 62.5 us -> 57.7 us  [per_device(): pl.pallas_call(kernel, out_shape=pltpu.VMEM((3, 2, 128), f32), in_specs=[...]
where the time goes in v2:
time: 59.1 us; the launch traced here: 59 us
  Pallas kernels  57.7 us (98%)
  between operations  0.66 us (1%)
    pallas_call x1, Pallas kernels, per_device(): pl.pallas_call(kernel, out_shape=pltpu.VMEM((3, 2, 128), f32), in_specs=[...  57.7 us

profile of v2, /device:TPU:1, one launch (start us, length us, event | category | flops | bytes accessed | tf_op | source)
XLA Modules:
  0.0 59.0 jit_solution(12827194619491046260)
XLA Ops:
  0.7 57.7 %shard_map.91 = f32[3,2,128]{2,1,0:T(2,128)S(1)} custom-call(f32[3,2,128]{2,1,0:T(2,128)} %bitcast.4, f32[2,128]{1,0:T(2,128)} %charges_in.1, s32[2]{0:T(128)} %counts_in.1, s32[2,128]{1,0:T(2,128)} %mols_in.1, s32[2,48]{1,0:T(2,128)} %bitcast.5, s32[1]{0:T(128)S(6)} %copy.12.listed_in, bf16[2,256,256]{2,1,0:T(8,128)(2,1)} %constant.6.clone.h_in, ...), custom_call_target="tpu_custom_call" | custom-call | tf_op jit(solution)/shard_map/pallas_call | solution.py:542
  58.4 0.6 copy.11

commit v3 on v2

--- a/solution.py
+++ b/solution.py
@@ -12,6 +12,8 @@
 
 GRID = 256
 N_DOM = 64
+RING_Y = 4
+RING_Z = 16
 N_PME = 8
 SX = 4
 SY = 32
@@ -143,8 +145,10 @@
     sp,
     rp,
     sd,
+    ta,
     rd,
     sd2,
+    tb,
     rd2,
     sq,
     rq,
@@ -156,10 +160,14 @@
     halo_r,
     p1_s,
     p1_r,
-    d1_s,
-    d1_r,
-    d2_s,
-    d2_r,
+    y1_s,
+    y1_r,
+    z1_s,
+    z1_r,
+    z2_s,
+    z2_r,
+    y2_s,
+    y2_r,
     p2_s,
     p2_r,
     f_s,
@@ -193,20 +201,29 @@
     for other in (up, down):
         pl.semaphore_signal(barrier, inc=1, device_id=(other, me_p), device_id_type=MESH)
 
-    def greet_pme(k, carry):
-        pl.semaphore_signal(
-            barrier, inc=1, device_id=(me_d, lax.rem(me_p + k, N_PME)), device_id_type=MESH
-        )
-        return carry
-
-    def greet_dom(k, carry):
-        pl.semaphore_signal(
-            barrier, inc=1, device_id=(lax.rem(me_d + k, N_DOM), me_p), device_id_type=MESH
-        )
-        return carry
-
-    lax.fori_loop(1, N_PME, greet_pme, 0)
-    lax.fori_loop(2, N_DOM - 1, greet_dom, 0)
+    def pme_at(k):
+        there = me_p + k
+        return jnp.where(there >= N_PME, there - N_PME, there)
+
+    me_z, me_y = me_d // RING_Y, me_d % RING_Y
+
+    def y_at(k):
+        there = me_y + k
+        return jnp.where(there >= RING_Y, there - RING_Y, there)
+
+    def z_at(k):
+        there = me_z + k
+        return jnp.where(there >= RING_Z, there - RING_Z, there)
+
+    for k in range(1, N_PME):
+        pl.semaphore_signal(barrier, inc=1, device_id=(me_d, pme_at(k)), device_id_type=MESH)
+
+    for k in range(1, RING_Y):
+        other = me_z * RING_Y + y_at(k)
+        pl.semaphore_signal(barrier, inc=1, device_id=(other, me_p), device_id_type=MESH)
+    for k in range(1, RING_Z):
+        other = z_at(k) * RING_Y + me_y
+        pl.semaphore_signal(barrier, inc=1, device_id=(other, me_p), device_id_type=MESH)
 
     for copy in inputs[:4]:
         copy.wait()
@@ -220,7 +237,7 @@
         at[1, b, 5:6, :] = live
         at[1, b, 6:8, :] = jnp.zeros((2, 128), f32)
 
-    pl.semaphore_wait(barrier, N_PME - 1 + N_DOM - 1)
+    pl.semaphore_wait(barrier, 2 + N_PME - 1 + RING_Y - 1 + RING_Z - 1)
 
     to_up = pltpu.make_async_remote_copy(
         src_ref=at.at[1],
@@ -301,7 +318,7 @@
             sp[4 * half + g] = piece
 
     def pme_copy(source, target, k, send, receive):
-        other = lax.rem(me_p + k, N_PME)
+        other = pme_at(k)
         return pltpu.make_async_remote_copy(
             src_ref=source.at[other],
             dst_ref=target.at[me_p],
@@ -317,25 +334,38 @@
             dst_ref=target.at[pl.ds(0, N_PME - 1)],
             send_sem=send,
             recv_sem=receive,
-            device_id=(me_d, lax.rem(me_p + 1, N_PME)),
+            device_id=(me_d, pme_at(1)),
             device_id_type=MESH,
         )
 
-    def dom_copy(source, target, k, send, receive):
-        other = lax.rem(me_d + k, N_DOM)
+    def start_y(source, target, send, receive):
+        for k in (2, 1, 3):
+            other = y_at(k)
+            pltpu.make_async_remote_copy(
+                src_ref=source(other),
+                dst_ref=target(me_y),
+                send_sem=send,
+                recv_sem=receive,
+                device_id=(me_z * RING_Y + other, me_p),
+                device_id_type=MESH,
+            ).start()
+
+    def start_z(source, target, send, receive):
+        for k in (8, 7, 9, 6, 10, 5, 11, 4, 12, 3, 13, 2, 14, 1, 15):
+            other = z_at(k)
+            pltpu.make_async_remote_copy(
+                src_ref=source(other),
+                dst_ref=target(me_z),
+                send_sem=send,
+                recv_sem=receive,
+                device_id=(other * RING_Y + me_y, me_p),
+                device_id_type=MESH,
+            ).start()
+
+    def all_of(view, send, receive):
         return pltpu.make_async_remote_copy(
-            src_ref=source.at[other],
-            dst_ref=target.at[me_d],
-            send_sem=send,
-            recv_sem=receive,
-            device_id=(other, me_p),
-            device_id_type=MESH,
-        )
-
-    def dom_all(source, target, send, receive):
-        return pltpu.make_async_remote_copy(
-            src_ref=source.at[pl.ds(0, N_DOM - 1)],
-            dst_ref=target.at[pl.ds(0, N_DOM - 1)],
+            src_ref=view,
+            dst_ref=view,
             send_sem=send,
             recv_sem=receive,
             device_id=(up, me_p),
@@ -343,21 +373,13 @@
         )
 
     def start_pme(source, target, send, receive):
-        def body(k, carry):
+        for k in (4, 3, 5, 2, 6, 7, 1):
             pme_copy(source, target, k, send, receive).start()
-            return carry
-
-        lax.fori_loop(1, N_PME, body, 0)
-
-    def start_dom(source, target, send, receive):
-        def body(k, carry):
-            dom_copy(source, target, N_DOM // 2 - k, send, receive).start()
-            dom_copy(source, target, N_DOM // 2 + k, send, receive).start()
-            return carry
-
-        dom_copy(source, target, N_DOM // 2, send, receive).start()
-        lax.fori_loop(1, N_DOM // 2, body, 0)
-
+
+    all_y1 = all_of(ta.at[pl.ds(0, RING_Y - 1)], y1_s, y1_r)
+    all_z1 = all_of(rd.at[pl.ds(0, RING_Z - 1)], z1_s, z1_r)
+    all_z2 = all_of(tb.at[pl.ds(0, RING_Z - 1)], z2_s, z2_r)
+    all_y2 = all_of(rd2.at[:, pl.ds(0, RING_Y - 1)], y2_s, y2_r)
     start_pme(sp, rp, p1_s, p1_r)
     rp[me_p] = sp[me_p]
 
@@ -372,8 +394,8 @@
     flat_sd = sd.reshape(GRID, 128)
     for x, piece in enumerate(swap_groups([lines[64 * k : 64 * (k + 1)] for k in range(4)])):
         flat_sd[pl.ds(x, 64, stride=4), :] = piece
-    start_dom(sd, rd, d1_s, d1_r)
-    rd[me_d] = sd[me_d]
+    start_y(lambda i: sd.at[:, i], lambda i: ta.at[i], y1_s, y1_r)
+    ta[me_y] = sd[:, me_y]
 
     def folded(index):
         return jnp.where(index < GRID // 2, index, index - GRID).astype(f32) * (1.0 / GRID)
@@ -388,11 +410,14 @@
         wave > 0.0, (recip_scale / GRID**3) * jnp.exp(-(math.pi**2) * safe) / safe, 0.0
     )
 
-    dom_all(sd, rd, d1_s, d1_r).wait_recv()
+    all_y1.wait_recv()
+    start_z(lambda i: ta.at[:, i], lambda i: rd.at[i], z1_s, z1_r)
+    rd[me_z] = ta[:, me_z]
+    all_z1.wait_recv()
     spectrum = product(table, split(rd.reshape(GRID, 128)[...])) * lam[...]
     sd2.reshape(GRID, 128)[...] = product(table, split(spectrum))
-    start_dom(sd2, rd2, d2_s, d2_r)
-    rd2[me_d] = sd2[me_d]
+    start_z(lambda i: sd2.at[i], lambda i: tb.at[i], z2_s, z2_r)
+    tb[me_z] = sd2[me_z]
 
     padded = jnp.concatenate([at[1, 0], at[1, 1], jnp.zeros((112, 128), f32)], axis=0)
     columns = padded.T
@@ -439,7 +464,10 @@
     )
     inputs[8].wait()
 
-    dom_all(sd2, rd2, d2_s, d2_r).wait_recv()
+    all_z2.wait_recv()
+    start_y(lambda i: tb.at[:, i], lambda i: rd2.at[:, i], y2_s, y2_r)
+    rd2[:, me_y] = tb[:, me_y]
+    all_y2.wait_recv()
     flat_rd2 = rd2.reshape(GRID, 128)
     lines = jnp.concatenate(
         swap_groups([flat_rd2[pl.ds(x, 64, stride=4), :] for x in range(4)]), axis=0
@@ -500,8 +528,8 @@
     to_up.wait_send()
     to_down.wait_send()
     pme_all(sp, rp, p1_s, p1_r).wait_send()
-    dom_all(sd, rd, d1_s, d1_r).wait_send()
-    dom_all(sd2, rd2, d2_s, d2_r).wait_send()
+    for copies in (all_y1, all_z1, all_z2, all_y2):
+        copies.wait_send()
     pme_all(sq, rq, p2_s, p2_r).wait_send()
     send_down.wait_recv()
     send_up.wait_recv()
@@ -562,10 +590,12 @@
             pltpu.VMEM((GRID, ATOMS), bf16),
             pltpu.VMEM((N_PME, ROWS_Y, 128), f32),
             pltpu.VMEM((N_PME, ROWS_Y, 128), f32),
-            pltpu.VMEM((N_DOM, 4, 128), f32),
-            pltpu.VMEM((N_DOM, 4, 128), f32),
-            pltpu.VMEM((N_DOM, 4, 128), f32),
-            pltpu.VMEM((N_DOM, 4, 128), f32),
+            pltpu.VMEM((RING_Z, RING_Y, 4, 128), f32),
+            pltpu.VMEM((RING_Y, RING_Z, 4, 128), f32),
+            pltpu.VMEM((RING_Z, RING_Y, 4, 128), f32),
+            pltpu.VMEM((RING_Z, RING_Y, 4, 128), f32),
+            pltpu.VMEM((RING_Z, RING_Y, 4, 128), f32),
+            pltpu.VMEM((RING_Z, RING_Y, 4, 128), f32),
             pltpu.VMEM((N_PME, ROWS_Y, 128), f32),
             pltpu.VMEM((N_PME, ROWS_Y, 128), f32),
             pltpu.VMEM((2, 8, 128), f32),
@@ -574,6 +604,10 @@
             pltpu.VMEM((2, 8, 128), f32),
             two,
             two,
+            one,
+            one,
+            one,
+            one,
             one,
             one,
             one,

time: 59.1 us -> 60.7 us (1.027)
  Pallas kernels: 57.7 us -> 59.4 us
    pallas_call x1, Pallas kernels: 57.7 us -> 59.4 us  [per_device(): pl.pallas_call(kernel, out_shape=pltpu.VMEM((3, 2, 128), f32), in_specs=[...]
where the time goes in v3:
time: 60.7 us; the launch traced here: 60.6 us
  Pallas kernels  59.4 us (98%)
  between operations  0.66 us (1%)
    pallas_call x1, Pallas kernels, per_device(): pl.pallas_call(kernel, out_shape=pltpu.VMEM((3, 2, 128), f32), in_specs=[...  59.4 us

profile of v3, /device:TPU:1, one launch (start us, length us, event | category | flops | bytes accessed | tf_op | source)
XLA Modules:
  0.0 60.6 jit_solution(7288228541427421133)
XLA Ops:
  0.7 59.4 %shard_map.91 = f32[3,2,128]{2,1,0:T(2,128)S(1)} custom-call(f32[3,2,128]{2,1,0:T(2,128)} %bitcast.4, f32[2,128]{1,0:T(2,128)} %charges_in.1, s32[2]{0:T(128)} %counts_in.1, s32[2,128]{1,0:T(2,128)} %mols_in.1, s32[2,48]{1,0:T(2,128)} %bitcast.5, s32[1]{0:T(128)S(6)} %copy.12.listed_in, bf16[2,256,256]{2,1,0:T(8,128)(2,1)} %constant.6.clone.h_in, ...), custom_call_target="tpu_custom_call" | custom-call | tf_op jit(solution)/shard_map/pallas_call | solution.py:570
  60.0 0.6 copy.11

commit v4 on v2

--- a/solution.py
+++ b/solution.py
@@ -12,6 +12,8 @@
 
 GRID = 256
 N_DOM = 64
+RING_Y = 4
+RING_Z = 16
 N_PME = 8
 SX = 4
 SY = 32
@@ -30,6 +32,8 @@
 
 SPANS = (((0, 144, 0), (240, 256, -256)), ((112, 256, 0), (0, 16, 256)))
 
+LANES = (256, 0, 512)
+
 NN = (((1,), (0,)), ((), ()))
 NT = (((1,), (1,)), ((), ()))
 
@@ -46,8 +50,12 @@
     return one(left[0], right[0]) + (one(left[0], right[1]) + one(left[1], right[0]))
 
 
+def lane_group(shape):
+    return lax.shift_right_logical(lax.broadcasted_iota(jnp.int32, shape, 1), 5)
+
+
 def swap_groups(pieces):
-    group = lax.broadcasted_iota(jnp.int32, pieces[0].shape, 1) // 32
+    group = lane_group((1, 128))
     out = []
     for j in range(4):
         total = pieces[j]
@@ -152,6 +160,7 @@
     fr,
     lam,
     short,
+    column_s,
     halo_s,
     halo_r,
     p1_s,
@@ -186,28 +195,55 @@
             )
         )
     ]
-    for copy in inputs:
+    for copy in inputs[:4]:
         copy.start()
 
     barrier = pltpu.get_barrier_semaphore()
     for other in (up, down):
         pl.semaphore_signal(barrier, inc=1, device_id=(other, me_p), device_id_type=MESH)
 
-    def greet_pme(k, carry):
+    def pme_at(k):
+        there = me_p + k
+        return jnp.where(there >= N_PME, there - N_PME, there)
+
+    def dom_at(k):
+        there = me_d + k
+        return jnp.where(there >= N_DOM, there - N_DOM, there)
+
+    def y_mate(k):
+        own_y = lax.rem(me_d, RING_Y)
+        return me_d - own_y + lax.rem(own_y + k, RING_Y)
+
+    for k in range(1, N_PME):
+        pl.semaphore_signal(barrier, inc=1, device_id=(me_d, pme_at(k)), device_id_type=MESH)
+
+    for k in range(1, RING_Y):
+        pl.semaphore_signal(barrier, inc=1, device_id=(y_mate(k), me_p), device_id_type=MESH)
+    for k in range(1, RING_Z):
         pl.semaphore_signal(
-            barrier, inc=1, device_id=(me_d, lax.rem(me_p + k, N_PME)), device_id_type=MESH
-        )
-        return carry
-
-    def greet_dom(k, carry):
-        pl.semaphore_signal(
-            barrier, inc=1, device_id=(lax.rem(me_d + k, N_DOM), me_p), device_id_type=MESH
-        )
-        return carry
-
-    lax.fori_loop(1, N_PME, greet_pme, 0)
-    lax.fori_loop(2, N_DOM - 1, greet_dom, 0)
-
+            barrier, inc=1, device_id=(dom_at(RING_Y * k), me_p), device_id_type=MESH
+        )
+
+    def far_first(visit, nearest):
+        visit(N_DOM // 2)
+        for j in range(1, 8):
+            visit(N_DOM // 2 - j)
+            visit(N_DOM // 2 + j)
+
+        def body(step, carry):
+            for j in range(8):
+                visit(N_DOM // 2 - 8 * step - j)
+                visit(N_DOM // 2 + 8 * step + j)
+            return carry
+
+        lax.fori_loop(1, 3, body, 0)
+        for j in range(24, N_DOM // 2 + 1 - nearest):
+            visit(N_DOM // 2 - j)
+            visit(N_DOM // 2 + j)
+
+
+    for copy in inputs[4:]:
+        copy.start()
     for copy in inputs[:4]:
         copy.wait()
     lane = lax.broadcasted_iota(jnp.int32, (1, 128), 1)
@@ -220,7 +256,7 @@
         at[1, b, 5:6, :] = live
         at[1, b, 6:8, :] = jnp.zeros((2, 128), f32)
 
-    pl.semaphore_wait(barrier, N_PME - 1 + N_DOM - 1)
+    pl.semaphore_wait(barrier, 2 + N_PME - 1 + RING_Y - 1 + RING_Z - 1)
 
     to_up = pltpu.make_async_remote_copy(
         src_ref=at.at[1],
@@ -240,10 +276,12 @@
     )
     to_up.start()
     to_down.start()
+    for k in range(1, RING_Y):
+        pl.semaphore_signal(column_s, inc=1, device_id=(y_mate(k), me_p), device_id_type=MESH)
 
     def fill(side, function, high_ref, low_ref):
         for b in range(2):
-            first = (2 * side + b) * 128
+            first = LANES[side] + 128 * b
             coord = at[side, b, 2:3, :]
             charge = at[side, b, 3:4, :]
             for start, stop, wrap_z in SPANS[b]:
@@ -256,7 +294,7 @@
     for refs in (wz_hi, wz_lo, dz_hi, dz_lo):
         for side in range(3):
             for b in range(2):
-                first = (2 * side + b) * 128
+                first = LANES[side] + 128 * b
                 refs[128 - 112 * b : 240 - 112 * b, first : first + 128] = jnp.zeros((112, 128), bf16)
     fill(1, weight, wz_hi, wz_lo)
     corner_x = (me_d * SX).astype(f32)
@@ -276,20 +314,22 @@
         flat_y = jnp.concatenate([at[side, b, 1:2, :] - corner_y for b in range(2)], axis=1)
         return flat_x - cells_x, flat_y - cells_y
 
-    def spread(side):
-        delta_x, delta_y = deltas(side)
-        wx, wy = weight(delta_x), weight(delta_y)
-        plane = jnp.concatenate([wx[x : x + 1] * wy for x in range(SX)], axis=0)
-        first = 256 * side
-        loaded = (wz_hi[:, first : first + 256], wz_lo[:, first : first + 256])
-        return product(split(plane), loaded, NT)
-
-    mesh = spread(1)
+    def spread(sides):
+        planes = []
+        for side in sides:
+            delta_x, delta_y = deltas(side)
+            wx, wy = weight(delta_x), weight(delta_y)
+            planes.append(jnp.concatenate([wx[x : x + 1] * wy for x in range(SX)], axis=0))
+        span = slice(LANES[sides[0]], LANES[sides[-1]] + 256)
+        loaded = (wz_hi[:, span], wz_lo[:, span])
+        return product(split(jnp.concatenate(planes, axis=1)), loaded, NT)
+
+    mesh = spread((1,))
     to_up.wait_recv()
     to_down.wait_recv()
-    for side in (0, 2):
-        fill(side, weight, wz_hi, wz_lo)
-        mesh = mesh + spread(side)
+    fill(0, weight, wz_hi, wz_lo)
+    fill(2, weight, wz_hi, wz_lo)
+    mesh = mesh + spread((0, 2))
     inputs[6].wait()
     table = (h[0], h[1])
     depth = product(split(mesh), table)
@@ -301,7 +341,7 @@
             sp[4 * half + g] = piece
 
     def pme_copy(source, target, k, send, receive):
-        other = lax.rem(me_p + k, N_PME)
+        other = pme_at(k)
         return pltpu.make_async_remote_copy(
             src_ref=source.at[other],
             dst_ref=target.at[me_p],
@@ -317,12 +357,12 @@
             dst_ref=target.at[pl.ds(0, N_PME - 1)],
             send_sem=send,
             recv_sem=receive,
-            device_id=(me_d, lax.rem(me_p + 1, N_PME)),
+            device_id=(me_d, pme_at(1)),
             device_id_type=MESH,
         )
 
     def dom_copy(source, target, k, send, receive):
-        other = lax.rem(me_d + k, N_DOM)
+        other = dom_at(k)
         return pltpu.make_async_remote_copy(
             src_ref=source.at[other],
             dst_ref=target.at[me_d],
@@ -343,20 +383,11 @@
         )
 
     def start_pme(source, target, send, receive):
-        def body(k, carry):
+        for k in (4, 3, 5, 2, 6, 7, 1):
             pme_copy(source, target, k, send, receive).start()
-            return carry
-
-        lax.fori_loop(1, N_PME, body, 0)
 
     def start_dom(source, target, send, receive):
-        def body(k, carry):
-            dom_copy(source, target, N_DOM // 2 - k, send, receive).start()
-            dom_copy(source, target, N_DOM // 2 + k, send, receive).start()
-            return carry
-
-        dom_copy(source, target, N_DOM // 2, send, receive).start()
-        lax.fori_loop(1, N_DOM // 2, body, 0)
+        far_first(lambda k: dom_copy(source, target, k, send, receive).start(), 1)
 
     start_pme(sp, rp, p1_s, p1_r)
     rp[me_p] = sp[me_p]
@@ -372,17 +403,17 @@
     flat_sd = sd.reshape(GRID, 128)
     for x, piece in enumerate(swap_groups([lines[64 * k : 64 * (k + 1)] for k in range(4)])):
         flat_sd[pl.ds(x, 64, stride=4), :] = piece
+    pl.semaphore_wait(column_s, RING_Y - 1)
     start_dom(sd, rd, d1_s, d1_r)
     rd[me_d] = sd[me_d]
 
     def folded(index):
         return jnp.where(index < GRID // 2, index, index - GRID).astype(f32) * (1.0 / GRID)
 
-    lanes = lax.broadcasted_iota(jnp.int32, (GRID, 128), 1)
     freq_x = folded(lax.broadcasted_iota(jnp.int32, (GRID, 128), 0))
-    freq_y = folded(me_d * 4 + lanes // 32)
-    freq_z = folded(me_p * 32 + lanes % 32)
-    wave = freq_x * freq_x + freq_y * freq_y + freq_z * freq_z
+    freq_y = folded(me_d * 4 + lane_group((1, 128)))
+    freq_z = folded(me_p * 32 + lane - 32 * lane_group((1, 128)))
+    wave = freq_x * freq_x + (freq_y * freq_y + freq_z * freq_z)
     safe = jnp.where(wave > 0.0, wave, 1.0)
     lam[...] = jnp.where(
         wave > 0.0, (recip_scale / GRID**3) * jnp.exp(-(math.pi**2) * safe) / safe, 0.0
@@ -434,9 +465,11 @@
         slopes_x.append(slope(delta_x))
         weights_y.append(weight(delta_y))
         slopes_y.append(slope(delta_y))
-    wx, dx, wy, dy = (
-        jnp.concatenate(parts, axis=1) for parts in (weights_x, slopes_x, weights_y, slopes_y)
-    )
+    for high_ref, low_ref in ((wz_hi, wz_lo), (dz_hi, dz_lo)):
+        high, low = split(product(table, (high_ref[...], low_ref[...])))
+        high_ref[...] = high
+        low_ref[...] = low
+
     inputs[8].wait()
 
     dom_all(sd2, rd2, d2_s, d2_r).wait_recv()
@@ -453,30 +486,28 @@
     depth = jnp.concatenate(
         [jnp.concatenate([halves[0][x], halves[1][x]], axis=1) for x in range(SX)], axis=0
     )
-    potential = split(product(split(depth), table))
-    along = product(potential, (wz_hi[...], wz_lo[...]))
-    along_slope = product(potential, (dz_hi[...], dz_lo[...]))
-    field = [0.0] * 3
-    for x in range(SX):
-        here = along[ROWS_Y * x : ROWS_Y * (x + 1)]
-        there = along_slope[ROWS_Y * x : ROWS_Y * (x + 1)]
-        field[0] = field[0] - dx[x : x + 1] * jnp.sum(wy * here, axis=0, keepdims=True)
-        field[1] = field[1] - wx[x : x + 1] * jnp.sum(dy * here, axis=0, keepdims=True)
-        field[2] = field[2] - wx[x : x + 1] * jnp.sum(wy * there, axis=0, keepdims=True)
+    lines = split(depth)
 
     def force_rows(side):
+        span = slice(LANES[side], LANES[side] + 256)
+        base = 32 if side == 2 else 0
+        spectrum = [part[base : base + (FLAT if side == 1 else 128)] for part in lines]
+        along = product(spectrum, (wz_hi[:, span], wz_lo[:, span]))
+        along_slope = product(spectrum, (dz_hi[:, span], dz_lo[:, span]))
+        wx, dx, wy, dy = weights_x[side], slopes_x[side], weights_y[side], slopes_y[side]
+        field = [0.0] * 3
+        for x in ((0, 1, 2), (0, 1, 2, 3), (1, 2, 3))[side]:
+            here = along[ROWS_Y * x - base : ROWS_Y * (x + 1) - base]
+            there = along_slope[ROWS_Y * x - base : ROWS_Y * (x + 1) - base]
+            field[0] = field[0] - dx[x : x + 1] * jnp.sum(wy * here, axis=0, keepdims=True)
+            field[1] = field[1] - wx[x : x + 1] * jnp.sum(dy * here, axis=0, keepdims=True)
+            field[2] = field[2] - wx[x : x + 1] * jnp.sum(wy * there, axis=0, keepdims=True)
         return jnp.concatenate(
-            [
-                field[v][:, 128 * (2 * side + b) : 128 * (2 * side + b + 1)]
-                for b in range(2)
-                for v in range(3)
-            ]
+            [field[v][:, 128 * b : 128 * (b + 1)] for b in range(2) for v in range(3)]
             + [jnp.zeros((2, 128), f32)],
             axis=0,
         )
 
-    fs[0] = force_rows(0)
-    fs[1] = force_rows(2) + short[1]
     send_down = pltpu.make_async_remote_copy(
         src_ref=fs.at[0],
         dst_ref=fr.at[0],
@@ -493,7 +524,9 @@
         device_id=(up, me_p),
         device_id_type=MESH,
     )
+    fs[0] = force_rows(0)
     send_down.start()
+    fs[1] = force_rows(2) + short[1]
     send_up.start()
     total = force_rows(1) + short[0]
 
@@ -572,6 +605,7 @@
             pltpu.VMEM((2, 8, 128), f32),
             pltpu.VMEM((GRID, 128), f32),
             pltpu.VMEM((2, 8, 128), f32),
+            pltpu.SemaphoreType.REGULAR,
             two,
             two,
             one,

time: 59.1 us -> 56.6 us (0.958)
  Pallas kernels: 57.7 us -> 55.3 us
    pallas_call x1, Pallas kernels: 57.7 us -> 55.3 us  [per_device(): pl.pallas_call(kernel, out_shape=pltpu.VMEM((3, 2, 128), f32), in_specs=[...]
where the time goes in v4:
time: 56.6 us; the launch traced here: 56.5 us
  Pallas kernels  55.3 us (98%)
  between operations  0.66 us (1%)
  local copies, waits for them, and re-layouts  0.58 us (1%)
    pallas_call x1, Pallas kernels, per_device(): pl.pallas_call(kernel, out_shape=pltpu.VMEM((3, 2, 128), f32), in_specs=[...  55.3 us

profile of v4, /device:TPU:1, one launch (start us, length us, event | category | flops | bytes accessed | tf_op | source)
XLA Modules:
  0.0 56.5 jit_solution(3803265045452242900)
XLA Ops:
  0.7 55.3 %shard_map.91 = f32[3,2,128]{2,1,0:T(2,128)S(1)} custom-call(f32[3,2,128]{2,1,0:T(2,128)} %bitcast.4, f32[2,128]{1,0:T(2,128)} %charges_in.1, s32[2]{0:T(128)} %counts_in.1, s32[2,128]{1,0:T(2,128)} %mols_in.1, s32[2,48]{1,0:T(2,128)} %bitcast.5, s32[1]{0:T(128)S(6)} %copy.12.listed_in, bf16[2,256,256]{2,1,0:T(8,128)(2,1)} %constant.6.clone.h_in, ...), custom_call_target="tpu_custom_call" | custom-call | tf_op jit(solution)/shard_map/pallas_call | solution.py:575
  55.9 0.6 %copy.11 = f32[2,3,128]{2,0,1:T(2,128)} copy(f32[2,3,128]{2,0,1:T(2,128)S(1)} %bitcast.3) | data formatting | bytes 6144

commit v5 on v4

--- a/solution.py
+++ b/solution.py
@@ -164,13 +164,15 @@
     halo_s,
     halo_r,
     p1_s,
-    p1_r,
+    p1_near,
+    p1_far,
     d1_s,
     d1_r,
     d2_s,
     d2_r,
     p2_s,
-    p2_r,
+    p2_near,
+    p2_far,
     f_s,
     f_r,
 ):
@@ -224,24 +226,6 @@
             barrier, inc=1, device_id=(dom_at(RING_Y * k), me_p), device_id_type=MESH
         )
 
-    def far_first(visit, nearest):
-        visit(N_DOM // 2)
-        for j in range(1, 8):
-            visit(N_DOM // 2 - j)
-            visit(N_DOM // 2 + j)
-
-        def body(step, carry):
-            for j in range(8):
-                visit(N_DOM // 2 - 8 * step - j)
-                visit(N_DOM // 2 + 8 * step + j)
-            return carry
-
-        lax.fori_loop(1, 3, body, 0)
-        for j in range(24, N_DOM // 2 + 1 - nearest):
-            visit(N_DOM // 2 - j)
-            visit(N_DOM // 2 + j)
-
-
     for copy in inputs[4:]:
         copy.start()
     for copy in inputs[:4]:
@@ -330,81 +314,97 @@
     fill(0, weight, wz_hi, wz_lo)
     fill(2, weight, wz_hi, wz_lo)
     mesh = mesh + spread((0, 2))
-    inputs[6].wait()
-    table = (h[0], h[1])
-    depth = product(split(mesh), table)
-    for half in range(2):
-        pieces = [
-            depth[ROWS_Y * x : ROWS_Y * (x + 1), 128 * half : 128 * (half + 1)] for x in range(SX)
-        ]
-        for g, piece in enumerate(swap_groups(pieces)):
-            sp[4 * half + g] = piece
-
-    def pme_copy(source, target, k, send, receive):
-        other = pme_at(k)
+    mesh = split(mesh)
+    own_half = me_p // 4
+    halves = (1 - own_half, own_half)
+
+    def send_half(source, target, half, first, send, receive):
+        for k in range(first, 4):
+            other = 4 * half + lax.rem(me_p + k, 4)
+            pltpu.make_async_remote_copy(
+                src_ref=source.at[other],
+                dst_ref=target.at[me_p],
+                send_sem=send,
+                recv_sem=receive,
+                device_id=(me_d, other),
+                device_id_type=MESH,
+            ).start()
+
+    def all_of(view, send, receive):
         return pltpu.make_async_remote_copy(
-            src_ref=source.at[other],
-            dst_ref=target.at[me_p],
-            send_sem=send,
-            recv_sem=receive,
-            device_id=(me_d, other),
-            device_id_type=MESH,
-        )
-
-    def pme_all(source, target, send, receive):
-        return pltpu.make_async_remote_copy(
-            src_ref=source.at[pl.ds(0, N_PME - 1)],
-            dst_ref=target.at[pl.ds(0, N_PME - 1)],
-            send_sem=send,
-            recv_sem=receive,
-            device_id=(me_d, pme_at(1)),
-            device_id_type=MESH,
-        )
-
-    def dom_copy(source, target, k, send, receive):
-        other = dom_at(k)
-        return pltpu.make_async_remote_copy(
-            src_ref=source.at[other],
-            dst_ref=target.at[me_d],
-            send_sem=send,
-            recv_sem=receive,
-            device_id=(other, me_p),
-            device_id_type=MESH,
-        )
-
-    def dom_all(source, target, send, receive):
-        return pltpu.make_async_remote_copy(
-            src_ref=source.at[pl.ds(0, N_DOM - 1)],
-            dst_ref=target.at[pl.ds(0, N_DOM - 1)],
+            src_ref=view,
+            dst_ref=view,
             send_sem=send,
             recv_sem=receive,
             device_id=(up, me_p),
             device_id_type=MESH,
         )
 
-    def start_pme(source, target, send, receive):
-        for k in (4, 3, 5, 2, 6, 7, 1):
-            pme_copy(source, target, k, send, receive).start()
-
-    def start_dom(source, target, send, receive):
-        far_first(lambda k: dom_copy(source, target, k, send, receive).start(), 1)
-
-    start_pme(sp, rp, p1_s, p1_r)
+    own_group, in_group = me_d // 16, lax.rem(me_d, 16)
+    far_groups = [lax.rem(own_group + k, 4) for k in (2, 1)]
+    near_groups = [lax.rem(own_group + k, 4) for k in (3, 0)]
+
+    def send_groups(source, target, groups, send, receive):
+        def one(other):
+            pltpu.make_async_remote_copy(
+                src_ref=source.at[other],
+                dst_ref=target.at[me_d],
+                send_sem=send,
+                recv_sem=receive,
+                device_id=(other, me_p),
+                device_id_type=MESH,
+            ).start()
+
+        def body(step, carry):
+            for j in range(4):
+                one(16 * groups[0] + 4 * step + j)
+            return carry
+
+        lax.fori_loop(0, 4, body, 0)
+        if groups is near_groups:
+            for k in range(1, 16):
+                one(16 * own_group + lax.rem(in_group + k, 16))
+        else:
+            def last(step, carry):
+                for j in range(4):
+                    one(16 * groups[1] + 4 * step + j)
+                return carry
+
+            lax.fori_loop(0, 4, last, 0)
+
+    inputs[6].wait()
+    for half in halves:
+        columns_z = pl.ds(pl.multiple_of(128 * half, 128), 128)
+        part = product(mesh, [h[i, :, :, columns_z].reshape(GRID, 128) for i in range(2)])
+        pieces = [part[ROWS_Y * x : ROWS_Y * (x + 1)] for x in range(SX)]
+        for g, piece in enumerate(swap_groups(pieces)):
+            sp[4 * half + g] = piece
+        if half is own_half:
+            send_half(sp, rp, half, 1, p1_s, p1_near)
+        else:
+            send_half(sp, rp, half, 0, p1_s, p1_far)
     rp[me_p] = sp[me_p]
 
     for side in range(3):
         fill(side, slope, dz_hi, dz_lo)
 
     inputs[7].wait()
-    pme_all(sp, rp, p1_s, p1_r).wait_recv()
-    lines = product(
-        (y[0], y[1]), split(rp[...].reshape(N_PME * ROWS_Y, 128))
-    )
+    all_of(rp.at[pl.ds(0, 3)], p1_s, p1_near).wait_recv()
+    all_of(rp.at[pl.ds(0, 4)], p1_s, p1_far).wait_recv()
+    received = split(rp[...].reshape(N_PME * ROWS_Y, 128))
+    pl.semaphore_wait(column_s, RING_Y - 1)
     flat_sd = sd.reshape(GRID, 128)
-    for x, piece in enumerate(swap_groups([lines[64 * k : 64 * (k + 1)] for k in range(4)])):
-        flat_sd[pl.ds(x, 64, stride=4), :] = piece
-    pl.semaphore_wait(column_s, RING_Y - 1)
-    start_dom(sd, rd, d1_s, d1_r)
+    for groups in (far_groups, near_groups):
+        rows_y = [jnp.concatenate([y[i, g] for g in groups], axis=0) for i in range(2)]
+        lines = product(rows_y, received)
+        pieces = [
+            jnp.concatenate([lines[16 * k : 16 * k + 16], lines[64 + 16 * k : 80 + 16 * k]], axis=0)
+            for k in range(4)
+        ]
+        for x, piece in enumerate(swap_groups(pieces)):
+            for i, g in enumerate(groups):
+                flat_sd[pl.ds(64 * g + x, 16, stride=4), :] = piece[16 * i : 16 * (i + 1)]
+        send_groups(sd, rd, groups, d1_s, d1_r)
     rd[me_d] = sd[me_d]
 
     def folded(index):
@@ -419,10 +419,21 @@
         wave > 0.0, (recip_scale / GRID**3) * jnp.exp(-(math.pi**2) * safe) / safe, 0.0
     )
 
-    dom_all(sd, rd, d1_s, d1_r).wait_recv()
-    spectrum = product(table, split(rd.reshape(GRID, 128)[...])) * lam[...]
-    sd2.reshape(GRID, 128)[...] = product(table, split(spectrum))
-    start_dom(sd2, rd2, d2_s, d2_r)
+    table = (h[0].reshape(GRID, GRID), h[1].reshape(GRID, GRID))
+    for high_ref, low_ref in ((wz_hi, wz_lo), (dz_hi, dz_lo)):
+        high, low = split(product(table, (high_ref[...], low_ref[...])))
+        high_ref[...] = high
+        low_ref[...] = low
+
+    all_of(rd.at[pl.ds(0, N_DOM - 1)], d1_s, d1_r).wait_recv()
+    spectrum = split(product(table, split(rd.reshape(GRID, 128)[...])) * lam[...])
+    flat_sd2 = sd2.reshape(GRID, 128)
+    for groups in (far_groups, near_groups):
+        rows_x = [jnp.concatenate([h[i, g] for g in groups], axis=0) for i in range(2)]
+        lines = product(rows_x, spectrum)
+        for i, g in enumerate(groups):
+            flat_sd2[pl.ds(pl.multiple_of(64 * g, 64), 64), :] = lines[64 * i : 64 * (i + 1)]
+        send_groups(sd2, rd2, groups, d2_s, d2_r)
     rd2[me_d] = sd2[me_d]
 
     padded = jnp.concatenate([at[1, 0], at[1, 1], jnp.zeros((112, 128), f32)], axis=0)
@@ -458,6 +469,24 @@
     short[0] = on_own.T[0:8]
     short[1] = jnp.concatenate(on_above[0] + on_above[1] + [jnp.zeros((2, 128), f32)], axis=0)
 
+    inputs[8].wait()
+
+    all_of(rd2.at[pl.ds(0, N_DOM - 1)], d2_s, d2_r).wait_recv()
+    flat_rd2 = rd2.reshape(GRID, 128)
+    lines = jnp.concatenate(
+        swap_groups([flat_rd2[pl.ds(x, 64, stride=4), :] for x in range(4)]), axis=0
+    )
+    lines = split(lines)
+    for half in halves:
+        part = product((yt[0, half], yt[1, half]), lines)
+        for g in range(4):
+            sq[4 * half + g] = part[ROWS_Y * g : ROWS_Y * (g + 1)]
+        if half is own_half:
+            send_half(sq, rq, half, 1, p2_s, p2_near)
+        else:
+            send_half(sq, rq, half, 0, p2_s, p2_far)
+    rq[me_p] = sq[me_p]
+
     weights_x, slopes_x, weights_y, slopes_y = [], [], [], []
     for side in range(3):
         delta_x, delta_y = deltas(side)
@@ -465,35 +494,27 @@
         slopes_x.append(slope(delta_x))
         weights_y.append(weight(delta_y))
         slopes_y.append(slope(delta_y))
-    for high_ref, low_ref in ((wz_hi, wz_lo), (dz_hi, dz_lo)):
-        high, low = split(product(table, (high_ref[...], low_ref[...])))
-        high_ref[...] = high
-        low_ref[...] = low
-
-    inputs[8].wait()
-
-    dom_all(sd2, rd2, d2_s, d2_r).wait_recv()
-    flat_rd2 = rd2.reshape(GRID, 128)
-    lines = jnp.concatenate(
-        swap_groups([flat_rd2[pl.ds(x, 64, stride=4), :] for x in range(4)]), axis=0
-    )
-    sq[...] = product((yt[0], yt[1]), split(lines)).reshape(N_PME, ROWS_Y, 128)
-    start_pme(sq, rq, p2_s, p2_r)
-    rq[me_p] = sq[me_p]
-
-    pme_all(sq, rq, p2_s, p2_r).wait_recv()
-    halves = [swap_groups([rq[4 * half + g] for g in range(4)]) for half in range(2)]
-    depth = jnp.concatenate(
-        [jnp.concatenate([halves[0][x], halves[1][x]], axis=1) for x in range(SX)], axis=0
-    )
-    lines = split(depth)
+    all_of(rq.at[pl.ds(0, 3)], p2_s, p2_near).wait_recv()
+    near = swap_groups([rq[4 * own_half + g] for g in range(4)])
+    all_of(rq.at[pl.ds(0, 4)], p2_s, p2_far).wait_recv()
+    far = swap_groups([rq[4 * (1 - own_half) + g] for g in range(4)])
+    lines = split(
+        jnp.concatenate(
+            [jnp.concatenate([near[x], far[x]], axis=1) for x in range(SX)], axis=0
+        )
+    )
+
+    def arrived(ref, span):
+        return jnp.concatenate(
+            [ref[pl.ds(pl.multiple_of(128 * half, 128), 128), span] for half in halves[::-1]], axis=0
+        )
 
     def force_rows(side):
         span = slice(LANES[side], LANES[side] + 256)
         base = 32 if side == 2 else 0
         spectrum = [part[base : base + (FLAT if side == 1 else 128)] for part in lines]
-        along = product(spectrum, (wz_hi[:, span], wz_lo[:, span]))
-        along_slope = product(spectrum, (dz_hi[:, span], dz_lo[:, span]))
+        along = product(spectrum, (arrived(wz_hi, span), arrived(wz_lo, span)))
+        along_slope = product(spectrum, (arrived(dz_hi, span), arrived(dz_lo, span)))
         wx, dx, wy, dy = weights_x[side], slopes_x[side], weights_y[side], slopes_y[side]
         field = [0.0] * 3
         for x in ((0, 1, 2), (0, 1, 2, 3), (1, 2, 3))[side]:
@@ -532,10 +553,10 @@
 
     to_up.wait_send()
     to_down.wait_send()
-    pme_all(sp, rp, p1_s, p1_r).wait_send()
-    dom_all(sd, rd, d1_s, d1_r).wait_send()
-    dom_all(sd2, rd2, d2_s, d2_r).wait_send()
-    pme_all(sq, rq, p2_s, p2_r).wait_send()
+    all_of(sp.at[pl.ds(0, N_PME - 1)], p1_s, p1_near).wait_send()
+    all_of(sd.at[pl.ds(0, N_DOM - 1)], d1_s, d1_r).wait_send()
+    all_of(sd2.at[pl.ds(0, N_DOM - 1)], d2_s, d2_r).wait_send()
+    all_of(sq.at[pl.ds(0, N_PME - 1)], p2_s, p2_near).wait_send()
     send_down.wait_recv()
     send_up.wait_recv()
     total = total + fr[0] + fr[1]
@@ -560,12 +581,17 @@
 def tables():
     index = np.arange(GRID)
     square = cas(index, index)
-    freq = (4 * np.arange(64)[None, :] + np.arange(4)[:, None]).reshape(-1)
+    freq = (64 * np.arange(4)[:, None, None] + np.arange(4)[:, None] + 4 * np.arange(16)).reshape(-1)
     cell = np.arange(ROWS_Y) - 3
     cells = (SY * np.arange(N_PME)[:, None] + cell[None, :]).reshape(-1)
     real = np.tile(np.arange(ROWS_Y) < SY + 6, N_PME)
     lines = cas(freq, cells % GRID) * real[None, :]
-    return [two_parts(square), two_parts(lines), two_parts(lines.T)]
+    turned = lines.reshape(4, 4, 16, -1).transpose(1, 0, 2, 3).reshape(GRID, -1).T
+    return [
+        two_parts(square).reshape(2, 4, 64, GRID),
+        two_parts(lines).reshape(2, 4, 64, -1),
+        two_parts(turned).reshape(2, 2, 4 * ROWS_Y, GRID),
+    ]
 
 
 def per_device(positions, charges, counts, mol_ids, pair_blocks, pair_count):
@@ -584,9 +610,9 @@
             pltpu.VMEM((2, 128), jnp.int32),
             pltpu.VMEM((2, 48), jnp.int32),
             pltpu.SMEM((1,), jnp.int32),
-            pltpu.VMEM((2, GRID, GRID), bf16),
-            pltpu.VMEM((2, GRID, N_PME * ROWS_Y), bf16),
-            pltpu.VMEM((2, N_PME * ROWS_Y, GRID), bf16),
+            pltpu.VMEM((2, 4, 64, GRID), bf16),
+            pltpu.VMEM((2, 4, 64, N_PME * ROWS_Y), bf16),
+            pltpu.VMEM((2, 2, 4 * ROWS_Y, GRID), bf16),
             pltpu.SemaphoreType.DMA((9,)),
             pltpu.VMEM((3, 2, 8, 128), f32),
             pltpu.VMEM((GRID, ATOMS), bf16),
@@ -616,6 +642,8 @@
             one,
             one,
             one,
+            one,
+            one,
             two,
             two,
         ],

time: 56.6 us -> 57 us (level)
  no operation moved by 1% of the time
where the time goes in v5:
time: 57 us; the launch traced here: 56.9 us
  Pallas kernels  55.6 us (98%)
  between operations  0.66 us (1%)
  local copies, waits for them, and re-layouts  0.58 us (1%)
    pallas_call x1, Pallas kernels, per_device(): pl.pallas_call(kernel, out_shape=pltpu.VMEM((3, 2, 128), f32), in_specs=[...  55.6 us

profile of v5, /device:TPU:1, one launch (start us, length us, event | category | flops | bytes accessed | tf_op | source)
XLA Modules:
  0.0 56.9 jit_solution(16459648530177761370)
XLA Ops:
  0.7 55.6 %shard_map.91 = f32[3,2,128]{2,1,0:T(2,128)S(1)} custom-call(f32[3,2,128]{2,1,0:T(2,128)} %bitcast.4, f32[2,128]{1,0:T(2,128)} %charges_in.1, s32[2]{0:T(128)} %counts_in.1, s32[2,128]{1,0:T(2,128)} %mols_in.1, s32[2,48]{1,0:T(2,128)} %bitcast.5, s32[1]{0:T(128)S(6)} %copy.12.listed_in, bf16[2,4,64,256]{3,2,1,0:T(8,128)(2,1)} %constant.6.clone.h_in, ...), custom_call_target="tpu_custom_call" | custom-call | tf_op jit(solution)/shard_map/pallas_call | solution.py:601
  56.3 0.6 %copy.11 = f32[2,3,128]{2,0,1:T(2,128)} copy(f32[2,3,128]{2,0,1:T(2,128)S(1)} %bitcast.3) | data formatting | bytes 6144

commit v6 on v5

--- a/solution.py
+++ b/solution.py
@@ -357,7 +357,7 @@
 
         def body(step, carry):
             for j in range(4):
-                one(16 * groups[0] + 4 * step + j)
+                one(16 * groups[0] + lax.rem(in_group + 4 * step + j, 16))
             return carry
 
         lax.fori_loop(0, 4, body, 0)
@@ -367,7 +367,7 @@
         else:
             def last(step, carry):
                 for j in range(4):
-                    one(16 * groups[1] + 4 * step + j)
+                    one(16 * groups[1] + lax.rem(in_group + 4 * step + j, 16))
                 return carry
 
             lax.fori_loop(0, 4, last, 0)

time: 57 us -> 56.4 us (0.989)
  Pallas kernels: 55.6 us -> 55 us
    pallas_call x1, Pallas kernels: 55.6 us -> 55 us  [per_device(): pl.pallas_call(kernel, out_shape=pltpu.VMEM((3, 2, 128), f32), in_specs=[...]
where the time goes in v6:
time: 56.4 us; the launch traced here: 56.2 us
  Pallas kernels  55 us (98%)
  between operations  0.66 us (1%)
  local copies, waits for them, and re-layouts  0.58 us (1%)
    pallas_call x1, Pallas kernels, per_device(): pl.pallas_call(kernel, out_shape=pltpu.VMEM((3, 2, 128), f32), in_specs=[...  55 us

profile of v6, /device:TPU:1, one launch (start us, length us, event | category | flops | bytes accessed | tf_op | source)
XLA Modules:
  0.0 56.2 jit_solution(5966489870291896016)
XLA Ops:
  0.7 55.0 %shard_map.91 = f32[3,2,128]{2,1,0:T(2,128)S(1)} custom-call(f32[3,2,128]{2,1,0:T(2,128)} %bitcast.4, f32[2,128]{1,0:T(2,128)} %charges_in.1, s32[2]{0:T(128)} %counts_in.1, s32[2,128]{1,0:T(2,128)} %mols_in.1, s32[2,48]{1,0:T(2,128)} %bitcast.5, s32[1]{0:T(128)S(6)} %copy.12.listed_in, bf16[2,4,64,256]{3,2,1,0:T(8,128)(2,1)} %constant.6.clone.h_in, ...), custom_call_target="tpu_custom_call" | custom-call | tf_op jit(solution)/shard_map/pallas_call | solution.py:601
  55.6 0.6 %copy.11 = f32[2,3,128]{2,0,1:T(2,128)} copy(f32[2,3,128]{2,0,1:T(2,128)S(1)} %bitcast.3) | data formatting | bytes 6144

commit v7 on v6

--- a/solution.py
+++ b/solution.py
@@ -341,8 +341,9 @@
         )
 
     own_group, in_group = me_d // 16, lax.rem(me_d, 16)
-    far_groups = [lax.rem(own_group + k, 4) for k in (2, 1)]
-    near_groups = [lax.rem(own_group + k, 4) for k in (3, 0)]
+    side = 1 + 2 * lax.rem(me_d // RING_Y, 2)
+    far_groups = [lax.rem(own_group + k, 4) for k in (2, side)]
+    near_groups = [lax.rem(own_group + k, 4) for k in (4 - side, 0)]
 
     def send_groups(source, target, groups, send, receive):
         def one(other):

time: 56.4 us -> 56.3 us (level)
  no operation moved by 1% of the time
where the time goes in v7:
time: 56.3 us; the launch traced here: 56.1 us
  Pallas kernels  54.9 us (98%)
  between operations  0.66 us (1%)
  local copies, waits for them, and re-layouts  0.58 us (1%)
    pallas_call x1, Pallas kernels, per_device(): pl.pallas_call(kernel, out_shape=pltpu.VMEM((3, 2, 128), f32), in_specs=[...  54.9 us

profile of v7, /device:TPU:1, one launch (start us, length us, event | category | flops | bytes accessed | tf_op | source)
XLA Modules:
  0.0 56.1 jit_solution(3653832192501375652)
XLA Ops:
  0.7 54.9 %shard_map.91 = f32[3,2,128]{2,1,0:T(2,128)S(1)} custom-call(f32[3,2,128]{2,1,0:T(2,128)} %bitcast.4, f32[2,128]{1,0:T(2,128)} %charges_in.1, s32[2]{0:T(128)} %counts_in.1, s32[2,128]{1,0:T(2,128)} %mols_in.1, s32[2,48]{1,0:T(2,128)} %bitcast.5, s32[1]{0:T(128)S(6)} %copy.12.listed_in, bf16[2,4,64,256]{3,2,1,0:T(8,128)(2,1)} %constant.6.clone.h_in, ...), custom_call_target="tpu_custom_call" | custom-call | tf_op jit(solution)/shard_map/pallas_call | solution.py:602
  55.5 0.6 %copy.11 = f32[2,3,128]{2,0,1:T(2,128)} copy(f32[2,3,128]{2,0,1:T(2,128)S(1)} %bitcast.3) | data formatting | bytes 6144

commit v8 on v6

--- a/solution.py
+++ b/solution.py
@@ -197,12 +197,11 @@
             )
         )
     ]
-    for copy in inputs[:4]:
-        copy.start()
-
     barrier = pltpu.get_barrier_semaphore()
     for other in (up, down):
         pl.semaphore_signal(barrier, inc=1, device_id=(other, me_p), device_id_type=MESH)
+    for copy in inputs[:4]:
+        copy.start()
 
     def pme_at(k):
         there = me_p + k
@@ -420,10 +419,13 @@
     )
 
     table = (h[0].reshape(GRID, GRID), h[1].reshape(GRID, GRID))
-    for high_ref, low_ref in ((wz_hi, wz_lo), (dz_hi, dz_lo)):
+
+    def transform(high_ref, low_ref):
         high, low = split(product(table, (high_ref[...], low_ref[...])))
         high_ref[...] = high
         low_ref[...] = low
+
+    transform(wz_hi, wz_lo)
 
     all_of(rd.at[pl.ds(0, N_DOM - 1)], d1_s, d1_r).wait_recv()
     spectrum = split(product(table, split(rd.reshape(GRID, 128)[...])) * lam[...])
@@ -469,6 +471,7 @@
     short[0] = on_own.T[0:8]
     short[1] = jnp.concatenate(on_above[0] + on_above[1] + [jnp.zeros((2, 128), f32)], axis=0)
 
+    transform(dz_hi, dz_lo)
     inputs[8].wait()
 
     all_of(rd2.at[pl.ds(0, N_DOM - 1)], d2_s, d2_r).wait_recv()

time: 56.4 us -> 56.4 us (level)
  no operation moved by 1% of the time
where the time goes in v8:
time: 56.4 us; the launch traced here: 56.2 us
  Pallas kernels  55 us (98%)
  between operations  0.66 us (1%)
  local copies, waits for them, and re-layouts  0.58 us (1%)
    pallas_call x1, Pallas kernels, per_device(): pl.pallas_call(kernel, out_shape=pltpu.VMEM((3, 2, 128), f32), in_specs=[...  55 us

profile of v8, /device:TPU:1, one launch (start us, length us, event | category | flops | bytes accessed | tf_op | source)
XLA Modules:
  0.0 56.2 jit_solution(250364323249329050)
XLA Ops:
  0.7 55.0 %shard_map.91 = f32[3,2,128]{2,1,0:T(2,128)S(1)} custom-call(f32[3,2,128]{2,1,0:T(2,128)} %bitcast.4, f32[2,128]{1,0:T(2,128)} %charges_in.1, s32[2]{0:T(128)} %counts_in.1, s32[2,128]{1,0:T(2,128)} %mols_in.1, s32[2,48]{1,0:T(2,128)} %bitcast.5, s32[1]{0:T(128)S(6)} %copy.12.listed_in, bf16[2,4,64,256]{3,2,1,0:T(8,128)(2,1)} %constant.6.clone.h_in, ...), custom_call_target="tpu_custom_call" | custom-call | tf_op jit(solution)/shard_map/pallas_call | solution.py:604
  55.7 0.6 %copy.11 = f32[2,3,128]{2,0,1:T(2,128)} copy(f32[2,3,128]{2,0,1:T(2,128)S(1)} %bitcast.3) | data formatting | bytes 6144
